TPU v7x, 32 devices: a whole 2x2x4 slice. The times are simulated.
32 devices in a mesh: dp: 8 (over z, y), mp: 4 (over x, core).
Axes of the slice: x: 2, y: 2, z: 4, core: 2. Of those that a mesh axis runs over, the one named last changes fastest.
Arguments:
- latents: float32 [8192, 16], P('dp'), may hold values from -6 to 6
- noise: float32 [8192, 16], P('dp'), may hold values from -6 to 6
- segment_ids: int32 [8192], P('dp'), may hold values from 0 to 3, as said below
- timesteps: int32 [8, 4], P('dp'), may hold values from 0 to 999
- labels: int32 [8, 4], P('dp'), may hold values from 0 to 1000
- w_qkv: float32 [768, 3, 768], P('dp', None, 'mp'), may hold values from -0.3125 to 0.3125
- w_out: float32 [768, 768], P('dp', 'mp'), may hold values from -0.625 to 0.625
- w_fc1: float32 [768, 3072], P('dp', 'mp'), may hold values from -0.21875 to 0.21875
- w_fc2: float32 [768, 3072], P('dp', 'mp'), may hold values from -0.109375 to 0.109375
- w_mod: float32 [768, 8, 768], P('dp', None, 'mp'), may hold values from -0.21875 to 0.21875
- w_head: float32 [768, 16], P('dp'), may hold values from -0.21875 to 0.21875
- w_cond: float32 [768, 2041], P('dp'), may hold values from -5 to 5
- mom_qkv: float32 [768, 3, 768], P('dp', None, 'mp'), may hold values from -0.00021362305 to 0.00021362305
- mom_out: float32 [768, 768], P('dp', 'mp'), may hold values from -0.00021362305 to 0.00021362305
- mom_fc1: float32 [768, 3072], P('dp', 'mp'), may hold values from -0.00021362305 to 0.00021362305
- mom_fc2: float32 [768, 3072], P('dp', 'mp'), may hold values from -0.00021362305 to 0.00021362305
- mom_mod: float32 [768, 8, 768], P('dp', None, 'mp'), may hold values from -0.00021362305 to 0.00021362305
- first_head: float32 [768, 16], P('dp'), may hold values from -2.2888184e-05 to 2.2888184e-05
- second_head: float32 [768, 16], P('dp'), may hold values from 9.718714e-12 to 3.9622448e-11
- first_cond: float32 [768, 2041], P('dp'), may hold values from -2.2888184e-05 to 2.2888184e-05
- second_cond: float32 [768, 2041], P('dp'), may hold values from 9.718714e-12 to 3.9622448e-11
Outputs:
- new_qkv: float32 [768, 3, 768], P('dp', None, 'mp')
- new_out: float32 [768, 768], P('dp', 'mp')
- new_fc1: float32 [768, 3072], P('dp', 'mp')
- new_fc2: float32 [768, 3072], P('dp', 'mp')
- new_mod: float32 [768, 8, 768], P('dp', None, 'mp')
- new_head: float32 [768, 16], P('dp')
- new_cond: float32 [768, 2041], P('dp')
- momentum_qkv: float32 [768, 3, 768], P('dp', None, 'mp')
- momentum_out: float32 [768, 768], P('dp', 'mp')
- momentum_fc1: float32 [768, 3072], P('dp', 'mp')
- momentum_fc2: float32 [768, 3072], P('dp', 'mp')
- momentum_mod: float32 [768, 8, 768], P('dp', None, 'mp')
- new_first_head: float32 [768, 16], P('dp')
- new_second_head: float32 [768, 16], P('dp')
- new_first_cond: float32 [768, 2041], P('dp')
- new_second_cond: float32 [768, 2041], P('dp')
- loss_sum: float32 [], replicated
- weight_total: float32 [], replicated
- grad_norm: float32 [], replicated
Inputs may be any that keep to these rules, and one draw needn't show every extreme that they name: `segment_ids`: each row of 1024 tokens is either one latent (all ids 0) or four latents of 256 tokens in order (ids 0, 1, 2, 3); at least one row holds four latents.
All inputs are finite; a program needn't handle non-finite values.
Results may differ from a plain program's by a relative error of at most 0.012.
Values may be sent and summed in bfloat16 or wider, within the bound.
No kernel may reach another device: no remote copies, remote signals or barrier semaphores. Data moves between devices by JAX's collectives and lax.ppermute only.
A program may use at most 256 MiB of HBM per device.

v0:
```python
import math

import jax
import jax.numpy as jnp
from jax import lax
from jax.sharding import PartitionSpec as P

SIDE = 32
D = 768
HEAD_DIM = 64
CLASSES = 1001
FREQ = 256
PIN = 16
STEP = 10


HIGH = lax.Precision.HIGHEST
GAMMA = 5.0
CLIP = 0.05
MU = 0.95
LR_MUON = 0.1
DECAY = 0.01
BETA_ONE = 0.9
BETA_TWO = 0.95
LR_ADAM = 0.08
EPS_ADAM = 1e-08
NS_COEF = (3.4445, -4.775, 2.0315)
ACROSS = (((1,), (1,)), ((), ()))
DOWN = (((0,), (0,)), ((), ()))


def plan():
    betas = jnp.linspace(0.0001, 0.02, 1000, dtype=jnp.float32)
    return jnp.cumprod(1.0 - betas)


def pick(table, index):
    grid = jnp.arange(table.shape[0], dtype=jnp.int32)
    return jnp.sum(jnp.where(index[..., None] == grid, table, 0.0), -1)


def normalize(x):
    mean = jnp.mean(x, -1, keepdims=True)
    cent = x - mean
    return cent * lax.rsqrt(jnp.mean(cent * cent, -1, keepdims=True) + 1e-06)


def modulate(x, shift, scale):
    return normalize(x) * (1.0 + scale) + shift


def positions(seg):
    length = seg.shape[-1]
    place = jnp.arange(length, dtype=jnp.int32)
    local = place - seg * (length // 4)
    side = jnp.where(jnp.max(seg, -1, keepdims=True) == 0, SIDE, SIDE // 2).astype(jnp.int32)
    down = (local // side).astype(jnp.float32)[..., None]
    across = (local % side).astype(jnp.float32)[..., None]
    quarter = D // 4
    omega = 1.0 / 10000.0 ** (jnp.arange(quarter, dtype=jnp.float32) / quarter)
    return jnp.concatenate(
        [
            jnp.sin(down * omega),
            jnp.cos(down * omega),
            jnp.sin(across * omega),
            jnp.cos(across * omega),
        ],
        -1,
    )


def time_features(steps):
    half = FREQ // 2
    freqs = jnp.exp(-math.log(10000.0) * jnp.arange(half, dtype=jnp.float32) / half)
    angles = steps.astype(jnp.float32)[:, None] * freqs
    return jnp.concatenate([jnp.cos(angles), jnp.sin(angles)], -1)


def orthogonal(block):
    if block.shape[0] > block.shape[1]:
        return orthogonal(block.T).T
    first, second, third = NS_COEF
    xmat = block / (jnp.sqrt(jnp.sum(block * block)) + 1e-07)
    for turn in range(5):
        gram = jnp.dot(xmat, xmat.T, precision=HIGH)
        poly = second * gram + third * jnp.dot(gram, gram, precision=HIGH)
        xmat = first * xmat + jnp.dot(poly, xmat, precision=HIGH)
    return xmat


def scaled_step(whole):
    flat = whole.reshape(whole.shape[0], -1)
    scale = 0.2 * math.sqrt(max(flat.shape))
    return (scale * orthogonal(flat)).reshape(whole.shape)


def empty_step(whole):
    return jnp.zeros_like(whole)


def split_heads(block):
    length = block.shape[0]
    return [block[:, kind].reshape(length, -1, HEAD_DIM) for kind in range(3)]


def masked_scores(query, key, seg):
    score = jnp.einsum(
        "qhd,khd->hqk", query, key, preferred_element_type=jnp.float32
    ) * HEAD_DIM ** (-0.5)
    return jnp.where((seg[:, None] == seg[None, :])[None], score, -1000000000.0)


def attend_rows(qkv_rows, seg_rows):

    def one(args):
        block, seg = args
        query, key, value = split_heads(block)
        score = masked_scores(query, key, seg)
        top = jnp.max(score, -1, keepdims=True)
        total = top + jnp.log(jnp.sum(jnp.exp(score - top), -1, keepdims=True))
        probs = jnp.exp(score - total).astype(jnp.bfloat16)
        mixed = jnp.einsum("hqk,khd->qhd", probs, value, preferred_element_type=jnp.float32)
        return (mixed.reshape(block.shape[0], -1), total)

    return lax.map(one, (qkv_rows, seg_rows))


def attend_back(qkv_rows, seg_rows, totals, grad_rows):

    def one(args):
        block, seg, total, grad = args
        length = block.shape[0]
        query, key, value = split_heads(block)
        probs = jnp.exp(masked_scores(query, key, seg) - total)
        grad_heads = grad.reshape(length, -1, HEAD_DIM)
        d_probs = jnp.einsum("qhd,khd->hqk", grad_heads, value, preferred_element_type=jnp.float32)
        d_value = jnp.einsum(
            "hqk,qhd->khd",
            probs.astype(jnp.bfloat16),
            grad_heads,
            preferred_element_type=jnp.float32,
        )
        delta = jnp.sum(d_probs * probs, -1, keepdims=True)
        d_score = (probs * (d_probs - delta) * HEAD_DIM ** (-0.5)).astype(jnp.bfloat16)
        d_query = jnp.einsum("hqk,khd->qhd", d_score, key, preferred_element_type=jnp.float32)
        d_key = jnp.einsum("hqk,qhd->khd", d_score, query, preferred_element_type=jnp.float32)
        return jnp.stack(
            [d_query.reshape(length, -1), d_key.reshape(length, -1), d_value.reshape(length, -1)], 1
        )

    return lax.map(one, (qkv_rows, seg_rows, totals, grad_rows))


def layer_forward(x_in, mods, seg_rows, weights):
    qkv_b, out_b, fc1_b, fc2_b = weights
    tokens = x_in.shape[0]
    rows = seg_rows.shape[0]
    h_in = modulate(x_in, mods[0], mods[1]).astype(jnp.bfloat16)
    qkv = jnp.einsum("td,dke->tke", h_in, qkv_b, preferred_element_type=jnp.float32).astype(
        jnp.bfloat16
    )
    qkv_rows = qkv.reshape(rows, tokens // rows, 3, qkv.shape[-1])
    mixed, totals = attend_rows(qkv_rows, seg_rows)
    mixed_b = mixed.reshape(tokens, -1).astype(jnp.bfloat16)
    attn = lax.psum(
        lax.dot_general(mixed_b, out_b, ACROSS, preferred_element_type=jnp.float32), "mp"
    )
    x_mid = x_in + mods[2] * attn
    h_mid = modulate(x_mid, mods[3], mods[4]).astype(jnp.bfloat16)
    upper = jnp.dot(h_mid, fc1_b, preferred_element_type=jnp.float32)
    act_b = jax.nn.gelu(upper, approximate=False).astype(jnp.bfloat16)
    mlp = lax.psum(lax.dot_general(act_b, fc2_b, ACROSS, preferred_element_type=jnp.float32), "mp")
    x_out = x_mid + mods[5] * mlp
    return (x_out, (h_in, qkv_rows, totals, mixed_b, attn, x_mid, h_mid, upper, act_b, mlp))


def layer_backward(d_out, x_in, mods, seg_rows, weights, kept):
    qkv_b, out_b, fc1_b, fc2_b = weights
    h_in, qkv_rows, totals, mixed_b, attn, x_mid, h_mid, upper, act_b, mlp = kept
    tokens = x_in.shape[0]
    rows = seg_rows.shape[0]
    d_mlp = (d_out * mods[5]).astype(jnp.bfloat16)
    d_gate2 = d_out * mlp
    d_fc2 = lax.dot_general(d_mlp, act_b, DOWN, preferred_element_type=jnp.float32)
    d_act = jnp.dot(d_mlp, fc2_b, preferred_element_type=jnp.float32)
    _, gelu_back = jax.vjp(lambda v: jax.nn.gelu(v, approximate=False), upper)
    d_upper = gelu_back(d_act)[0].astype(jnp.bfloat16)
    d_fc1 = lax.dot_general(h_mid, d_upper, DOWN, preferred_element_type=jnp.float32)
    d_hmid = lax.psum(
        lax.dot_general(d_upper, fc1_b, ACROSS, preferred_element_type=jnp.float32), "mp"
    )
    _, mid_back = jax.vjp(modulate, x_mid, mods[3], mods[4])
    dx_mid, d_shift2, d_scale2 = mid_back(d_hmid)
    d_mid = d_out + dx_mid
    d_attn = (d_mid * mods[2]).astype(jnp.bfloat16)
    d_gate1 = d_mid * attn
    d_outw = lax.dot_general(d_attn, mixed_b, DOWN, preferred_element_type=jnp.float32)
    d_mixed = jnp.dot(d_attn, out_b, preferred_element_type=jnp.float32).astype(jnp.bfloat16)
    d_qkv = attend_back(qkv_rows, seg_rows, totals, d_mixed.reshape(rows, tokens // rows, -1))
    d_qkv = d_qkv.reshape(tokens, 3, -1).astype(jnp.bfloat16)
    d_wqkv = jnp.einsum("td,tke->dke", h_in, d_qkv, preferred_element_type=jnp.float32)
    d_hin = lax.psum(
        jnp.einsum("tke,dke->td", d_qkv, qkv_b, preferred_element_type=jnp.float32), "mp"
    )
    _, in_back = jax.vjp(modulate, x_in, mods[0], mods[1])
    dx_in, d_shift1, d_scale1 = in_back(d_hin)
    d_mods = [d_shift1, d_scale1, d_gate1, d_shift2, d_scale2, d_gate2]
    return (d_mid + dx_in, d_mods, (d_wqkv, d_outw, d_fc1, d_fc2))


def body(
    latents,
    noise,
    segment_ids,
    timesteps,
    labels,
    w_qkv,
    w_out,
    w_fc1,
    w_fc2,
    w_mod,
    w_head,
    w_cond,
    mom_qkv,
    mom_out,
    mom_fc1,
    mom_fc2,
    mom_mod,
    first_head,
    second_head,
    first_cond,
    second_cond,
):
    low_type = jnp.bfloat16
    qkv_b, out_b, fc1_b, fc2_b, mod_b, head_b, cond_b = (
        lax.all_gather(w_qkv.astype(low_type), "dp", axis=0, tiled=True),
        lax.all_gather(w_out.astype(low_type), "dp", axis=0, tiled=True),
        lax.all_gather(w_fc1.astype(low_type), "dp", axis=0, tiled=True),
        lax.all_gather(w_fc2.astype(low_type), "dp", axis=0, tiled=True),
        lax.all_gather(w_mod.astype(low_type), "dp", axis=0, tiled=True),
        lax.all_gather(w_head.astype(low_type), "dp", axis=0, tiled=True),
        lax.all_gather(w_cond.astype(low_type), "dp", axis=0, tiled=True),
    )
    moms = (mom_qkv, mom_out, mom_fc1, mom_fc2, mom_mod)
    tokens = latents.shape[0]
    rows = timesteps.shape[0]
    length = tokens // rows
    seg_rows = segment_ids.reshape(rows, length)
    steps = timesteps.reshape(-1)
    abar = pick(plan(), steps)
    snr = abar / (1.0 - abar)
    slot_weight = jnp.minimum(snr, GAMMA) / snr
    slot_of = jnp.arange(tokens, dtype=jnp.int32) // length * 4 + segment_ids
    select = (slot_of[:, None] == jnp.arange(4 * rows, dtype=jnp.int32)).astype(jnp.float32)
    abar_tok = jnp.dot(select, abar, precision=HIGH)
    weight_tok = jnp.dot(select, slot_weight, precision=HIGH)
    noisy_b = (
        jnp.sqrt(abar_tok)[:, None] * latents + jnp.sqrt(1.0 - abar_tok)[:, None] * noise
    ).astype(low_type)
    w_patch = cond_b[:, :PIN]
    w_time1 = cond_b[:, PIN : PIN + FREQ]
    w_time2 = cond_b[:, PIN + FREQ : PIN + FREQ + D]
    table = cond_b[:, PIN + FREQ + D :]
    x_in = lax.dot_general(
        noisy_b, w_patch, ACROSS, preferred_element_type=jnp.float32
    ) + positions(seg_rows).reshape(tokens, -1)
    feat_b = time_features(steps).astype(low_type)
    hidden_t = lax.dot_general(feat_b, w_time1, ACROSS, preferred_element_type=jnp.float32)
    silu_t_b = jax.nn.silu(hidden_t).astype(low_type)
    time_emb = lax.dot_general(silu_t_b, w_time2, ACROSS, preferred_element_type=jnp.float32)
    onehot = (labels.reshape(-1)[:, None] == jnp.arange(CLASSES, dtype=jnp.int32)).astype(
        jnp.float32
    )
    cond = time_emb + lax.dot_general(
        onehot.astype(low_type), table, ACROSS, preferred_element_type=jnp.float32
    )
    silu_c_b = jax.nn.silu(cond).astype(low_type)
    mod_cols = jnp.einsum("sd,dke->ske", silu_c_b, mod_b, preferred_element_type=jnp.float32)
    mod = lax.all_gather(mod_cols, "mp", axis=2, tiled=True)
    mods = [jnp.dot(select, mod[:, k], precision=HIGH) for k in range(8)]
    weights = (qkv_b, out_b, fc1_b, fc2_b)
    x_out, kept = layer_forward(x_in, mods, seg_rows, weights)
    h_fin = modulate(x_out, mods[6], mods[7]).astype(low_type)
    pred = jnp.dot(h_fin, head_b, preferred_element_type=jnp.float32)
    diff = pred - noise
    err = jnp.sum(diff * diff, -1)
    loss_sum, weight_total = lax.psum((jnp.sum(weight_tok * err), jnp.sum(weight_tok)), "dp")
    d_err = weight_tok / weight_total
    d_pred = (2.0 * diff * d_err[:, None]).astype(low_type)
    d_head = lax.dot_general(h_fin, d_pred, DOWN, preferred_element_type=jnp.float32)
    d_hfin = lax.dot_general(d_pred, head_b, ACROSS, preferred_element_type=jnp.float32)
    _, fin_back = jax.vjp(modulate, x_out, mods[6], mods[7])
    d_xout, d_shiftf, d_scalef = fin_back(d_hfin)
    d_x, d_mods, layer_grads = layer_backward(d_xout, x_in, mods, seg_rows, weights, kept)
    d_mods = d_mods + [d_shiftf, d_scalef]
    d_mod = jnp.stack(
        [lax.dot_general(select, piece, DOWN, precision=HIGH) for piece in d_mods], 1
    ).astype(low_type)
    width = mod_b.shape[-1]
    d_mod_cols = lax.dynamic_slice_in_dim(d_mod, lax.axis_index("mp") * width, width, 2)
    d_wmod = jnp.einsum("sd,ske->dke", silu_c_b, d_mod_cols, preferred_element_type=jnp.float32)
    d_silu_c = lax.psum(
        jnp.einsum("ske,dke->sd", d_mod_cols, mod_b, preferred_element_type=jnp.float32), "mp"
    )
    _, silu_c_back = jax.vjp(jax.nn.silu, cond)
    d_cond = silu_c_back(d_silu_c)[0]
    d_table = jnp.einsum("sd,sk->dk", d_cond, onehot, precision=HIGH)
    d_time2 = jnp.einsum("sd,se->de", d_cond, silu_t_b.astype(jnp.float32), precision=HIGH)
    d_silu_t = jnp.einsum("sd,de->se", d_cond, w_time2.astype(jnp.float32), precision=HIGH)
    _, silu_t_back = jax.vjp(jax.nn.silu, hidden_t)
    d_hidden_t = silu_t_back(d_silu_t)[0]
    d_time1 = jnp.einsum("sd,sf->df", d_hidden_t, feat_b.astype(jnp.float32), precision=HIGH)
    d_patch = lax.dot_general(
        d_x.astype(low_type), noisy_b, DOWN, preferred_element_type=jnp.float32
    )
    d_condw = jnp.concatenate([d_patch, d_time1, d_time2, d_table], 1)
    d_wqkv, d_outw, d_fc1, d_fc2 = layer_grads
    shards = (
        lax.psum_scatter(d_wqkv, "dp", scatter_dimension=0, tiled=True),
        lax.psum_scatter(d_outw, "dp", scatter_dimension=0, tiled=True),
        lax.psum_scatter(d_fc1, "dp", scatter_dimension=0, tiled=True),
        lax.psum_scatter(d_fc2, "dp", scatter_dimension=0, tiled=True),
        lax.psum_scatter(d_wmod, "dp", scatter_dimension=0, tiled=True),
        lax.psum_scatter(d_head, "dp", scatter_dimension=0, tiled=True),
        lax.psum_scatter(d_condw, "dp", scatter_dimension=0, tiled=True),
    )
    split_sq = sum((jnp.sum(g * g) for g in shards[:5]))
    copied_sq = sum((jnp.sum(g * g) for g in shards[5:]))
    split_sq, copied_sq = lax.psum((split_sq, copied_sq), ("dp", "mp"))
    grad_norm = jnp.sqrt(split_sq + copied_sq / lax.axis_size("mp"))
    coef = jnp.minimum(1.0, CLIP / (grad_norm + 1e-06))
    new_moms = tuple((MU * m + coef * g for m, g in zip(moms, shards[:5])))
    full_moms = (
        lax.all_gather(new_moms[0], "dp", axis=0, tiled=True),
        lax.all_gather(new_moms[1], "dp", axis=0, tiled=True),
        lax.all_gather(new_moms[2], "dp", axis=0, tiled=True),
        lax.all_gather(new_moms[3], "dp", axis=0, tiled=True),
        lax.all_gather(new_moms[4], "dp", axis=0, tiled=True),
    )
    masters = (w_qkv, w_out, w_fc1, w_fc2, w_mod)
    spread = max(1, lax.axis_size("dp") // 5)
    device_rank = lax.axis_index("dp")
    owned = [
        lax.cond(device_rank == number * spread, scaled_step, empty_step, whole)
        for number, whole in enumerate(full_moms)
    ]
    my_steps = (
        lax.psum_scatter(
            owned[0].astype(jnp.bfloat16), "dp", scatter_dimension=0, tiled=True
        ).astype(jnp.float32),
        lax.psum_scatter(
            owned[1].astype(jnp.bfloat16), "dp", scatter_dimension=0, tiled=True
        ).astype(jnp.float32),
        lax.psum_scatter(
            owned[2].astype(jnp.bfloat16), "dp", scatter_dimension=0, tiled=True
        ).astype(jnp.float32),
        lax.psum_scatter(
            owned[3].astype(jnp.bfloat16), "dp", scatter_dimension=0, tiled=True
        ).astype(jnp.float32),
        lax.psum_scatter(
            owned[4].astype(jnp.bfloat16), "dp", scatter_dimension=0, tiled=True
        ).astype(jnp.float32),
    )
    new_weights = [
        master * (1.0 - LR_MUON * DECAY) - LR_MUON * mine for master, mine in zip(masters, my_steps)
    ]
    adam_out = []
    for master, first, second, grad in (
        (w_head, first_head, second_head, shards[5]),
        (w_cond, first_cond, second_cond, shards[6]),
    ):
        clipped = coef * grad
        first = BETA_ONE * first + (1.0 - BETA_ONE) * clipped
        second = BETA_TWO * second + (1.0 - BETA_TWO) * clipped * clipped
        update = (
            first / (1.0 - BETA_ONE**STEP) / (jnp.sqrt(second / (1.0 - BETA_TWO**STEP)) + EPS_ADAM)
        )
        adam_out.append((master - LR_ADAM * (update + DECAY * master), first, second))
    return (
        new_weights[0],
        new_weights[1],
        new_weights[2],
        new_weights[3],
        new_weights[4],
        adam_out[0][0],
        adam_out[1][0],
        new_moms[0],
        new_moms[1],
        new_moms[2],
        new_moms[3],
        new_moms[4],
        adam_out[0][1],
        adam_out[0][2],
        adam_out[1][1],
        adam_out[1][2],
        loss_sum,
        weight_total,
        grad_norm,
    )


def solution(mesh):
    in_specs = (
        P("dp", None),
        P("dp", None),
        P("dp"),
        P("dp", None),
        P("dp", None),
        P("dp", None, "mp"),
        P("dp", "mp"),
        P("dp", "mp"),
        P("dp", "mp"),
        P("dp", None, "mp"),
        P("dp", None),
        P("dp", None),
        P("dp", None, "mp"),
        P("dp", "mp"),
        P("dp", "mp"),
        P("dp", "mp"),
        P("dp", None, "mp"),
        P("dp", None),
        P("dp", None),
        P("dp", None),
        P("dp", None),
    )
    out_specs = (
        P("dp", None, "mp"),
        P("dp", "mp"),
        P("dp", "mp"),
        P("dp", "mp"),
        P("dp", None, "mp"),
        P("dp", None),
        P("dp", None),
        P("dp", None, "mp"),
        P("dp", "mp"),
        P("dp", "mp"),
        P("dp", "mp"),
        P("dp", None, "mp"),
        P("dp", None),
        P("dp", None),
        P("dp", None),
        P("dp", None),
        P(),
        P(),
        P(),
    )
    return jax.shard_map(body, mesh=mesh, in_specs=in_specs, out_specs=out_specs, check_vma=False)
```

profile of v0, /device:TPU:0, one launch (start us, length us, event | category | flops | bytes accessed | tf_op | source)
XLA Modules:
  0.0 1937.8 jit_solution(6036854576334225575)
XLA Ops:
  13.5 43.7 %all_gather.57 = bf16[768,3,192]{2,1,0:T(4,128)(2,1)S(1)} all-gather(bf16[96,3,192]{2,1,0:T(4,128)(2,1)S(1)} %copy.296), channel_id=1, replica_groups=mesh['dp'=8,'mp'=4] {'dp'}, dimensions={0}, use_global_device_ids=true | all-gather | bytes 995328 | tf_op jit(solution)/shard_map/all_gather | solution.py:236
  59.7 34.3 %all_gather.58 = bf16[768,192]{1,0:T(8,128)(2,1)} all-gather(bf16[96,192]{1,0:T(8,128)(2,1)S(1)} %convert_element_type.173), channel_id=1, replica_groups=mesh['dp'=8,'mp'=4] {'dp'}, dimensions={0}, use_global_device_ids=true | all-gather | bytes 331776 | tf_op jit(solution)/shard_map/all_gather | solution.py:237
  108.8 46.9 %all-gather.12.cloned.1.call-done = bf16[768,8,192]{2,0,1:T(8,128)(2,1)} async-done(((bf16[96,8,192]{2,0,1:T(8,128)(2,1)}), bf16[768,8,192]{2,0,1:T(8,128)(2,1)}) %all-gather.12.cloned.1.call-update) | async-done | bytes 2359312 | tf_op jit(solution)/shard_map/all_gather | solution.py:240
  219.8 54.6 %all-reduce.8.cloned.1.call-done = f32[1024,768]{0,1:T(8,128)} async-done(((f32[1024,768]{0,1:T(8,128)}), f32[1024,768]{0,1:T(8,128)}) %all-reduce.8.cloned.1.call-update) | async-done | bytes 3145744 | tf_op jit(solution)/shard_map/psum | solution.py:165
  285.7 32.5 %all-gather.14.cloned.1.call-done = bf16[768,768]{1,0:T(8,128)(2,1)} async-done(((bf16[96,768]{1,0:T(8,128)(2,1)}), bf16[768,768]{1,0:T(8,128)(2,1)}) %all-gather.14.cloned.1.call-update) | async-done | bytes 1179664 | tf_op jit(solution)/shard_map/all_gather | solution.py:238
  329.5 31.1 %all-gather.16.cloned.1.call-done = bf16[768,768]{1,0:T(8,128)(2,1)} async-done(((bf16[96,768]{1,0:T(8,128)(2,1)}), bf16[768,768]{1,0:T(8,128)(2,1)}) %all-gather.16.cloned.1.call-update) | async-done | bytes 1179664 | tf_op jit(solution)/shard_map/all_gather | solution.py:239
  366.1 30.4 %all-gather = bf16[8,96,16]{1,2,0:T(8,128)(2,1)S(1)} all-gather(bf16[1,96,16]{1,2,0:T(8,128)(2,1)S(1)} %convert_bitcast_fusion), channel_id=1, replica_groups=mesh['dp'=8,'mp'=4] {'dp'}, dimensions={0}, use_global_device_ids=true | all-gather | bytes 27648 | tf_op jit(solution)/shard_map/all_gather | solution.py:241
  486.5 65.0 %all-reduce.12.cloned.1.call-done = f32[1024,768]{0,1:T(8,128)} async-done(((f32[1024,768]{0,1:T(8,128)}), f32[1024,768]{0,1:T(8,128)}) %all-reduce.12.cloned.1.call-update) | async-done | bytes 3145744 | tf_op jit(solution)/shard_map/psum | solution.py:189
  646.2 47.5 %all-reduce.14.cloned.1.call-done = f32[1024,768]{0,1:T(8,128)} async-done(((f32[1024,768]{0,1:T(8,128)}), f32[1024,768]{0,1:T(8,128)}) %all-reduce.14.cloned.1.call-update) | async-done | bytes 3145744 | tf_op jit(solution)/shard_map/psum | solution.py:202
  760.0 63.8 %reduce-scatter.25.cloned.1.call-done = f32[96,192]{1,0:T(8,128)} async-done(((f32[768,192]{1,0:T(8,128)}), f32[96,192]{1,0:T(8,128)}) %reduce-scatter.25.cloned.1.call-update) | async-done | bytes 73744 | tf_op jit(solution)/shard_map/reduce_scatter | solution.py:320
  825.3 70.5 %reduce-scatter.29.cloned.1.call-done = f32[96,768]{1,0:T(8,128)} async-done(((f32[768,768]{1,0:T(8,128)}), f32[96,768]{1,0:T(8,128)}) %reduce-scatter.29.cloned.1.call-update) | async-done | bytes 294928 | tf_op jit(solution)/shard_map/reduce_scatter | solution.py:322
  897.5 70.2 %reduce-scatter.27.cloned.1.call-done = f32[96,768]{1,0:T(8,128)} async-done(((f32[768,768]{1,0:T(8,128)}), f32[96,768]{1,0:T(8,128)}) %reduce-scatter.27.cloned.1.call-update) | async-done | bytes 294928 | tf_op jit(solution)/shard_map/reduce_scatter | solution.py:321
  969.3 70.3 %reduce-scatter.23.cloned.1.call-done = f32[96,3,192]{2,0,1:T(8,128)} async-done(((f32[768,3,192]{2,0,1:T(8,128)}), f32[96,3,192]{2,0,1:T(8,128)}) %reduce-scatter.23.cloned.1.call-update) | async-done | bytes 221200 | tf_op jit(solution)/shard_map/reduce_scatter | solution.py:319
  1043.9 116.6 %reduce-scatter.31.cloned.1.call-done = f32[96,8,192]{2,0,1:T(8,128)} async-done(((f32[768,8,192]{2,0,1:T(8,128)}), f32[96,8,192]{2,0,1:T(8,128)}) %reduce-scatter.31.cloned.1.call-update) | async-done | bytes 589840 | tf_op jit(solution)/shard_map/reduce_scatter | solution.py:323
  1163.1 118.4 %reduce-scatter.39.cloned.1.call-done = f32[96,2041]{1,0:T(8,128)} async-done(((f32[768,2041]{1,0:T(8,128)}), f32[96,2041]{1,0:T(8,128)}) %reduce-scatter.39.cloned.1.call-update) | async-done | bytes 783760 | tf_op jit(solution)/shard_map/reduce_scatter | solution.py:325
  1285.2 39.8 %all-reduce.1 = (f32[]{:T(128)}, f32[]{:T(128)}) all-reduce(f32[]{:T(128)S(6)} %add.448, f32[]{:T(128)S(6)} %add.450), channel_id=1, replica_groups=mesh['dp'=8,'mp'=4] {'dp','mp'}, use_global_device_ids=true, to_apply=%region_33.34 | all-reduce | flops 2 | bytes 16 | tf_op jit(solution)/shard_map/psum | solution.py:329
  1333.2 33.0 %all_gather.63 = f32[768,192]{1,0:T(8,128)S(1)} all-gather(f32[96,192]{1,0:T(8,128)S(1)} %multiply_add_fusion.36), channel_id=1, replica_groups=mesh['dp'=8,'mp'=4] {'dp'}, dimensions={0}, use_global_device_ids=true | all-gather | bytes 663552 | tf_op jit(solution)/shard_map/all_gather | solution.py:335
  1384.4 76.5 %conditional.5 = (bf16[768,3,192]{0,2,1:T(8,128)(2,1)S(1)}) conditional(s32[]{:T(128)} %convert_element_type.155, () %tuple.45, f32[768,3,192]{2,0,1:T(8,128)} %all-gather.18.cloned.1.call-done), branch_computations={%region_42.43_spmd, %region_43.45_spmd} | conditional | flops 42061344768 | bytes 90685480 | solution.py:344
  1502.8 90.2 %all-gather.24.cloned.1.call-done = f32[768,8,192]{2,0,1:T(8,128)} async-done(((f32[96,8,192]{2,0,1:T(8,128)}), f32[768,8,192]{2,0,1:T(8,128)}) %all-gather.24.cloned.1.call-update) | async-done | bytes 4718608 | tf_op jit(solution)/shard_map/all_gather | solution.py:338
  1606.9 49.9 %reduce-scatter.43.cloned.1.call-done = bf16[96,192]{1,0:T(8,128)(2,1)} async-done(((bf16[768,192]{1,0:T(8,128)(2,1)}), bf16[96,192]{1,0:T(8,128)(2,1)}) %reduce-scatter.43.cloned.1.call-update) | async-done | bytes 36880
  1658.4 64.5 %reduce-scatter.41.cloned.1.call-done = bf16[96,576]{1,0:T(8,128)(2,1)} async-done(((bf16[768,576]{1,0:T(8,128)(2,1)}), bf16[96,576]{1,0:T(8,128)(2,1)}) %reduce-scatter.41.cloned.1.call-update) | async-done | bytes 110608
  1724.9 64.5 %reduce-scatter.35.cloned.1.call-done = bf16[96,768]{1,0:T(8,128)(2,1)} async-done(((bf16[768,768]{1,0:T(8,128)(2,1)}), bf16[96,768]{1,0:T(8,128)(2,1)}) %reduce-scatter.35.cloned.1.call-update) | async-done | bytes 147472 | tf_op jit(solution)/shard_map/reduce_scatter | solution.py:357
  1791.0 64.8 %reduce-scatter.33.cloned.1.call-done = bf16[96,768]{1,0:T(8,128)(2,1)} async-done(((bf16[768,768]{1,0:T(8,128)(2,1)}), bf16[96,768]{1,0:T(8,128)(2,1)}) %reduce-scatter.33.cloned.1.call-update) | async-done | bytes 147472 | tf_op jit(solution)/shard_map/reduce_scatter | solution.py:354
  1857.5 69.6 %reduce-scatter.45.cloned.1.call-done = bf16[96,1536]{1,0:T(8,128)(2,1)} async-done(((bf16[768,1536]{1,0:T(8,128)(2,1)}), bf16[96,1536]{1,0:T(8,128)(2,1)}) %reduce-scatter.45.cloned.1.call-update) | async-done | bytes 294928
  (469 shorter events, 538.7 us)
Async XLA Ops:
  7.2 96.2 %all-gather.10.cloned.1.call-start = ((), (), s32[]{:S(2)}) async-start(), calls=%async_computation.12 | async-start | bytes 3538944 | tf_op jit(solution)/shard_map/all_gather | solution.py:242
  9.3 146.5 %all-gather.12.cloned.1.call-start = ((), (), s32[]{:S(2)}) async-start(), calls=%async_computation.13 | async-start | bytes 3538944 | tf_op jit(solution)/shard_map/all_gather | solution.py:240
  11.4 262.9 %all-reduce.8.cloned.1.call-start = ((), (), s32[]{:S(2)}) async-start(), calls=%async_computation.14 | async-start | bytes 6291456 | tf_op jit(solution)/shard_map/psum | solution.py:165
  207.4 110.7 %all-gather.14.cloned.1.call-start = ((), (), s32[]{:S(2)}) async-start(), calls=%async_computation.15 | async-start | bytes 1327104 | tf_op jit(solution)/shard_map/all_gather | solution.py:238
  209.3 151.3 %all-gather.16.cloned.1.call-start = ((), (), s32[]{:S(2)}) async-start(), calls=%async_computation.16 | async-start | bytes 1327104 | tf_op jit(solution)/shard_map/all_gather | solution.py:239
  211.0 221.8 %all-reduce.10.cloned.1.call-start = ((), (), s32[]{:S(2)}) async-start(), calls=%async_computation.17 | async-start | bytes 6291456 | tf_op jit(solution)/shard_map/psum | solution.py:172
  365.5 186.0 %all-reduce.12.cloned.1.call-start = ((), (), s32[]{:S(2)}) async-start(), calls=%async_computation.18 | async-start | bytes 6291456 | tf_op jit(solution)/shard_map/psum | solution.py:189
  486.4 207.2 %all-reduce.14.cloned.1.call-start = ((), (), s32[]{:S(2)}) async-start(), calls=%async_computation.23 | async-start | bytes 6291456 | tf_op jit(solution)/shard_map/psum | solution.py:202
  624.9 133.5 %reduce-scatter.37.cloned.1.call-start = ((), (), s32[]{:S(2)}) async-start(), calls=%async_computation.31 | async-start | bytes 442368
  627.8 196.0 %reduce-scatter.25.cloned.1.call-start = ((), (), s32[]{:S(2)}) async-start(), calls=%async_computation.20 | async-start | bytes 884736 | tf_op jit(solution)/shard_map/reduce_scatter | solution.py:320
  630.8 265.0 %reduce-scatter.29.cloned.1.call-start = ((), (), s32[]{:S(2)}) async-start(), calls=%async_computation.22 | async-start | bytes 2654208 | tf_op jit(solution)/shard_map/reduce_scatter | solution.py:322
  635.6 332.0 %reduce-scatter.27.cloned.1.call-start = ((), (), s32[]{:S(2)}) async-start(), calls=%async_computation.21 | async-start | bytes 2654208 | tf_op jit(solution)/shard_map/reduce_scatter | solution.py:321
  640.5 399.1 %reduce-scatter.23.cloned.1.call-start = ((), (), s32[]{:S(2)}) async-start(), calls=%async_computation.19 | async-start | bytes 2654208 | tf_op jit(solution)/shard_map/reduce_scatter | solution.py:319
  645.9 514.6 %reduce-scatter.31.cloned.1.call-start = ((), (), s32[]{:S(2)}) async-start(), calls=%async_computation.24 | async-start | bytes 7077888 | tf_op jit(solution)/shard_map/reduce_scatter | solution.py:323
  718.1 563.4 %reduce-scatter.39.cloned.1.call-start = ((), (), s32[]{:S(2)}) async-start(), calls=%async_computation.32 | async-start | bytes 7077888 | tf_op jit(solution)/shard_map/reduce_scatter | solution.py:325
  753.3 631.1 %all-gather.18.cloned.1.call-start = ((), (), s32[]{:S(2)}) async-start(), calls=%async_computation.25 | async-start | bytes 2654208 | tf_op jit(solution)/shard_map/all_gather | solution.py:334
  1328.1 134.2 %all-gather.22.cloned.1.call-start = ((), (), s32[]{:S(2)}) async-start(), calls=%async_computation.28 | async-start | bytes 2654208 | tf_op jit(solution)/shard_map/all_gather | solution.py:337
  1329.9 162.5 %all-gather.20.cloned.1.call-start = ((), (), s32[]{:S(2)}) async-start(), calls=%async_computation.26 | async-start | bytes 2654208 | tf_op jit(solution)/shard_map/all_gather | solution.py:336
  1331.8 261.3 %all-gather.24.cloned.1.call-start = ((), (), s32[]{:S(2)}) async-start(), calls=%async_computation.30 | async-start | bytes 7077888 | tf_op jit(solution)/shard_map/all_gather | solution.py:338
  1333.1 323.7 %reduce-scatter.43.cloned.1.call-start = ((), (), s32[]{:S(2)}) async-start(), calls=%async_computation.34 | async-start | bytes 442368
  1367.1 355.8 %reduce-scatter.41.cloned.1.call-start = ((), (), s32[]{:S(2)}) async-start(), calls=%async_computation.33 | async-start | bytes 1105920
  1462.2 327.1 %reduce-scatter.35.cloned.1.call-start = ((), (), s32[]{:S(2)}) async-start(), calls=%async_computation.29 | async-start | bytes 1327104 | tf_op jit(solution)/shard_map/reduce_scatter | solution.py:357
  1479.2 376.6 %reduce-scatter.33.cloned.1.call-start = ((), (), s32[]{:S(2)}) async-start(), calls=%async_computation.27 | async-start | bytes 1327104 | tf_op jit(solution)/shard_map/reduce_scatter | solution.py:354
  1502.8 424.3 %reduce-scatter.45.cloned.1.call-start = ((), (), s32[]{:S(2)}) async-start(), calls=%async_computation.35 | async-start | bytes 2654208
  (115 other events, 2608.2 us)
Sparse Core Ops, SparseCore 0:
  10.2 83.6 all-gather.9
  96.7 59.0 all-gather.11
  207.5 66.7 all-reduce.7
  276.9 41.1 all-gather.13
  320.8 39.8 all-gather.15
  365.6 67.1 all-reduce.9
  486.5 64.8 all-reduce.11
  625.1 68.5 all-reduce.13
  696.9 61.5 reduce-scatter.36
  762.2 61.5 reduce-scatter.24
  827.7 68.0 reduce-scatter.28
  899.6 68.0 reduce-scatter.26
  971.5 67.9 reduce-scatter.22
  1043.4 117.0 reduce-scatter.30
  1164.4 117.1 reduce-scatter.38
  1328.3 56.0 all-gather.17
  1387.2 51.6 all-gather.21
  1441.8 50.5 all-gather.19
  1495.5 97.5 all-gather.23
  1597.1 59.5 reduce-scatter.42
  1660.4 62.4 reduce-scatter.40
  1726.3 63.0 reduce-scatter.34
  1792.8 62.9 reduce-scatter.32
  1859.2 67.9 reduce-scatter.44
where the time goes:
time: 1950 us; the launch traced here: 1940 us
  waiting for transfers between devices  1250 us (64%)
  matrix products  261 us (13%)
  blocking collectives  227 us (12%)
  local copies, waits for them, and re-layouts  76.9 us (4%)
  other arithmetic  67.8 us (3%)
  loops' own time  32.1 us (2%)
  between operations  23.7 us (1%)
    unnamed x28, waiting for transfers between devices  190 us
    reduce_scatter x1, waiting for transfers between devices, body(): lax.psum_scatter(d_condw, 'dp', scatter_dimension=0, tiled=True)  118 us
    reduce_scatter x1, waiting for transfers between devices, body(): lax.psum_scatter(d_wmod, 'dp', scatter_dimension=0, tiled=True)  117 us
    all_gather x1, waiting for transfers between devices, body(): lax.all_gather(new_moms[4], 'dp', axis=0, tiled=True)  90.2 us
    reduce_scatter x1, waiting for transfers between devices, body(): lax.psum_scatter(d_fc2, 'dp', scatter_dimension=0, tiled=True)  70.5 us
    reduce_scatter x1, waiting for transfers between devices, body(): lax.psum_scatter(d_wqkv, 'dp', scatter_dimension=0, tiled=True)  70.3 us
    reduce_scatter x1, waiting for transfers between devices, body(): lax.psum_scatter(d_fc1, 'dp', scatter_dimension=0, tiled=True)  70.2 us
    psum x1, waiting for transfers between devices, layer_backward(): lax.psum(lax.dot_general(d_upper, fc1_b, ACROSS, preferred_element_type=j...  65 us
  transfers between devices with their start and end apart: 24, of which 22 were waited for; matrix products, arithmetic and copies ran while one was open for 12% of the time, Pallas kernels for 0%

commit v1 on v0

v1 whole, which is shorter than its diff:
```python
import math

import jax
import jax.numpy as jnp
from jax import lax
from jax.sharding import PartitionSpec as P

SIDE = 32
D = 768
HEAD_DIM = 64
CLASSES = 1001
FREQ = 256
PIN = 16
STEP = 10
SLOTS = 4

HIGH = lax.Precision.HIGHEST
GAMMA = 5.0
CLIP = 0.05
MU = 0.95
LR_MUON = 0.1
DECAY = 0.01
BETA_ONE = 0.9
BETA_TWO = 0.95
LR_ADAM = 0.08
EPS_ADAM = 1e-08
NS_COEF = (3.4445, -4.775, 2.0315)
NS_SHIFT = (0.0, 0.1, 0.5, 0.8, 0.8)
ACROSS = (((1,), (1,)), ((), ()))
DOWN = (((0,), (0,)), ((), ()))
ALONG = (((1,), (0,)), ((), ()))
LOW = jnp.bfloat16
F32 = jnp.float32


def dot(a, b, dims=ALONG):
    return lax.dot_general(a, b, dims, preferred_element_type=F32)


def swap(x, axis, bit):
    size = lax.axis_size(axis)
    return lax.ppermute(x, axis, [(i, i ^ bit) for i in range(size)])


def gather_rows(x, axis):
    size = lax.axis_size(axis)
    me = lax.axis_index(axis)
    cur = x[None]
    bit = size // 2
    while bit >= 1:
        other = swap(cur, axis, bit)
        low_half = (me // bit) % 2 == 0
        cur = jnp.where(low_half, jnp.stack([cur, other], 1), jnp.stack([other, cur], 1))
        cur = cur.reshape((-1,) + x.shape)
        bit //= 2
    return cur.reshape((-1,) + x.shape[1:])


def scatter_sum(x, axis):
    size = lax.axis_size(axis)
    me = lax.axis_index(axis)
    cur = x.reshape((size, x.shape[0] // size) + x.shape[1:])
    bit = 1
    while bit < size:
        pair = cur.reshape((cur.shape[0] // 2, 2) + cur.shape[1:])
        mine = (me // bit) % 2
        keep = lax.dynamic_index_in_dim(pair, mine, 1, keepdims=False)
        send = lax.dynamic_index_in_dim(pair, 1 - mine, 1, keepdims=False)
        cur = keep.astype(F32) + swap(send.astype(LOW), axis, bit).astype(F32)
        bit *= 2
    return cur[0]


def spread(x, axis):
    size = lax.axis_size(axis)
    copies = jnp.broadcast_to(x[None], (size,) + x.shape)
    return lax.all_to_all(copies, axis, 0, 0, tiled=True)


def exchange(x, axis):
    return lax.all_to_all(x, axis, 0, 0, tiled=True)


def plan():
    betas = jnp.linspace(0.0001, 0.02, 1000, dtype=F32)
    return jnp.cumprod(1.0 - betas)


def pick(table, index):
    grid = jnp.arange(table.shape[0], dtype=jnp.int32)
    return jnp.sum(jnp.where(index[..., None] == grid, table, 0.0), -1)


def normalize(x):
    cent = x - jnp.mean(x, -1, keepdims=True)
    inv = lax.rsqrt(jnp.mean(cent * cent, -1, keepdims=True) + 1e-06)
    return cent * inv, inv


def norm_back(grad, unit, inv, scale):
    d_shift = jnp.sum(grad, 0)
    d_scale = jnp.sum(grad * unit, 0)
    g = grad * (1.0 + scale)
    dx = inv * (g - jnp.mean(g, -1, keepdims=True) - unit * jnp.mean(g * unit, -1, keepdims=True))
    return dx, d_shift, d_scale


def positions(single, part, rank, length):
    quarter = D // 4
    omega = 1.0 / 10000.0 ** (jnp.arange(quarter, dtype=F32) / quarter)
    angle = jnp.arange(SIDE, dtype=F32)[:, None] * omega
    sin, cos = jnp.sin(angle), jnp.cos(angle)
    half = SIDE // 2
    rows = part // SIDE

    def spans(table):
        first = lax.dynamic_slice_in_dim(table, rank * rows, rows, 0)
        down_one = jnp.broadcast_to(first[:, None], (rows, SIDE, quarter)).reshape(part, quarter)
        down_four = jnp.broadcast_to(table[:half, None], (half, half, quarter)).reshape(part, quarter)
        across_one = jnp.broadcast_to(table[None], (rows, SIDE, quarter)).reshape(part, quarter)
        across_four = jnp.broadcast_to(table[None, :half], (half, half, quarter)).reshape(part, quarter)
        return jnp.where(single, down_one, down_four), jnp.where(single, across_one, across_four)

    sin_down, sin_across = spans(sin)
    cos_down, cos_across = spans(cos)
    return jnp.concatenate([sin_down, cos_down, sin_across, cos_across], -1)


def time_features(steps):
    half = FREQ // 2
    freqs = jnp.exp(-math.log(10000.0) * jnp.arange(half, dtype=F32) / half)
    angles = steps.astype(F32)[:, None] * freqs
    return jnp.concatenate([jnp.cos(angles), jnp.sin(angles)], -1)


def silu_slope(x):
    s = jax.nn.sigmoid(x)
    return s * (1.0 + x * (1.0 - s))


def heads_of(block):
    return block.reshape(block.shape[0], -1, HEAD_DIM).transpose(1, 0, 2)


def rows_of(block):
    return block.transpose(1, 0, 2).reshape(block.shape[1], -1)


def masked_scores(query, key, seg):
    score = jnp.einsum("hqd,hkd->hqk", query, key, preferred_element_type=F32) * HEAD_DIM ** (-0.5)
    return jnp.where((seg[:, None] == seg[None, :])[None], score, -1000000000.0)


def attend(query, key, value, seg):
    score = masked_scores(query, key, seg)
    top = jnp.max(score, -1, keepdims=True)
    total = top + jnp.log(jnp.sum(jnp.exp(score - top), -1, keepdims=True))
    probs = jnp.exp(score - total).astype(LOW)
    mixed = jnp.einsum("hqk,hkd->hqd", probs, value, preferred_element_type=F32)
    return mixed, total


def attend_back(query, key, value, seg, total, grad):
    probs = jnp.exp(masked_scores(query, key, seg) - total)
    d_probs = jnp.einsum("hqd,hkd->hqk", grad, value, preferred_element_type=F32)
    d_value = jnp.einsum("hqk,hqd->hkd", probs.astype(LOW), grad, preferred_element_type=F32)
    delta = jnp.sum(d_probs * probs, -1, keepdims=True)
    d_score = (probs * (d_probs - delta) * HEAD_DIM ** (-0.5)).astype(LOW)
    d_query = jnp.einsum("hqk,hkd->hqd", d_score, key, preferred_element_type=F32)
    d_key = jnp.einsum("hqk,hqd->hkd", d_score, query, preferred_element_type=F32)
    return d_query, d_key, d_value


def orthogonal_rows(whole, own, count):
    first, second, third = NS_COEF
    wide = whole.shape[0] <= whole.shape[1]
    x = whole / (jnp.sqrt(jnp.sum(whole * whole)) + 1e-07)
    size = min(whole.shape)
    eye = jnp.eye(size, dtype=F32)
    last = len(NS_SHIFT) - 1
    for turn, shift in enumerate(NS_SHIFT):
        xb = x.astype(LOW)
        gram = dot(xb, xb, ACROSS if wide else DOWN) - shift * eye
        gb = gram.astype(LOW)
        centre = first + second * shift + third * shift * shift
        slope = second + 2.0 * third * shift
        if turn == last:
            x = lax.dynamic_slice_in_dim(x, own, count, 0)
            if wide:
                mine = lax.dynamic_slice_in_dim(gram, own, count, 0)
                poly = slope * mine + third * dot(mine.astype(LOW), gb)
                return centre * x + dot(poly.astype(LOW), xb)
            poly = slope * gram + third * dot(gb, gb)
            return centre * x + dot(x.astype(LOW), poly.astype(LOW))
        poly = (slope * gram + third * dot(gb, gb)).astype(LOW)
        x = centre * x + (dot(poly, xb) if wide else dot(xb, poly))


def body(
    latents,
    noise,
    segment_ids,
    timesteps,
    labels,
    w_qkv,
    w_out,
    w_fc1,
    w_fc2,
    w_mod,
    w_head,
    w_cond,
    mom_qkv,
    mom_out,
    mom_fc1,
    mom_fc2,
    mom_mod,
    first_head,
    second_head,
    first_cond,
    second_cond,
):
    n_dp, n_mp = lax.axis_size("dp"), lax.axis_size("mp")
    me, rank = lax.axis_index("dp"), lax.axis_index("mp")
    tokens = latents.shape[0]
    part = tokens // n_mp
    rows = w_qkv.shape[0]
    width = w_qkv.shape[2]
    hidden = w_fc1.shape[1]

    qkv_b = gather_rows(w_qkv.reshape(rows, -1).astype(LOW), "dp")
    rest = gather_rows(jnp.concatenate([w_out, w_fc1, w_fc2], 1).astype(LOW), "dp")
    out_b, fc1_b, fc2_b = rest[:, :width], rest[:, width : width + hidden], rest[:, width + hidden :]

    single = jnp.max(segment_ids) == 0
    note = jnp.concatenate(
        [
            timesteps.reshape(-1).astype(F32),
            labels.reshape(-1).astype(F32),
            single.astype(F32)[None],
            jnp.zeros((2 * PIN - 2 * SLOTS - 1,), F32),
        ]
    )
    thin = jnp.concatenate([w_cond[:, :PIN], w_head], 1)
    packet = spread(jnp.concatenate([thin, jnp.broadcast_to(note, (8, 2 * PIN))], 0), "dp")
    packet = packet.reshape(n_dp, rows + 8, 2 * PIN)
    thin_b = packet[:, :rows].reshape(n_dp * rows, 2 * PIN).astype(LOW)
    patch_b, head_b = thin_b[:, :PIN], thin_b[:, PIN:]
    notes = packet[:, rows]
    steps = notes[:, :SLOTS].astype(jnp.int32)
    kinds = notes[:, SLOTS : 2 * SLOTS].astype(jnp.int32).reshape(-1)
    singles = notes[:, 2 * SLOTS] > 0.5

    abar = pick(plan(), steps)
    snr = abar / (1.0 - abar)
    slot_weight = jnp.minimum(snr, GAMMA) / snr
    weight_total = part * jnp.sum(jnp.where(singles[:, None], n_mp * slot_weight[:, :1] / SLOTS, slot_weight))

    time1_b = w_cond[:, PIN : PIN + FREQ].astype(LOW)
    time2_b = w_cond[:, PIN + FREQ : PIN + FREQ + D].astype(LOW)
    table_b = w_cond[:, PIN + FREQ + D :].astype(LOW)
    mod_b = w_mod.reshape(rows, -1).astype(LOW)
    feat_b = time_features(steps.reshape(-1)).astype(LOW)
    slots_all = feat_b.shape[0]
    hidden_t = dot(feat_b, time1_b, ACROSS)
    silu_t = spread(jax.nn.silu(hidden_t).astype(LOW), "dp").reshape(n_dp, slots_all, rows)
    silu_t_b = silu_t.transpose(1, 0, 2).reshape(slots_all, n_dp * rows)
    onehot = (kinds[:, None] == jnp.arange(CLASSES, dtype=jnp.int32)).astype(F32)
    cond = dot(silu_t_b, time2_b, ACROSS) + dot(onehot.astype(LOW), table_b, ACROSS)
    silu_c_b = jax.nn.silu(cond).astype(LOW)
    mod_part = dot(silu_c_b, mod_b).reshape(n_dp, SLOTS, -1)
    mod_cols = jnp.sum(exchange(mod_part, "dp"), 0).reshape(SLOTS, 8, width)
    mod = lax.all_gather(mod_cols, "mp", axis=2, tiled=True)
    slot = lax.dynamic_index_in_dim(segment_ids, rank * part, 0, keepdims=False)
    mods = lax.dynamic_index_in_dim(mod, slot, 0, keepdims=False)

    my_row = lambda a: lax.dynamic_index_in_dim(a, me, 0, keepdims=False)
    my_slot = lambda a: lax.dynamic_index_in_dim(my_row(a), slot, 0, keepdims=False)
    abar_tok, weight_tok = my_slot(abar), my_slot(slot_weight)
    lat = lax.dynamic_slice_in_dim(latents, rank * part, part, 0)
    noi = lax.dynamic_slice_in_dim(noise, rank * part, part, 0)
    noisy_b = (jnp.sqrt(abar_tok) * lat + jnp.sqrt(1.0 - abar_tok) * noi).astype(LOW)
    x_in = dot(noisy_b, patch_b, ACROSS) + positions(single, part, rank, tokens)
    unit1, inv1 = normalize(x_in)
    h_in = gather_rows((unit1 * (1.0 + mods[1]) + mods[0]).astype(LOW), "mp")

    qkv = dot(h_in, qkv_b).astype(LOW)
    query, key, value = (heads_of(qkv[:, k * width : (k + 1) * width]) for k in range(3))
    mixed, totals = attend(query, key, value, segment_ids)
    mixed_b = rows_of(mixed.astype(LOW))
    attn = scatter_sum(dot(mixed_b, out_b, ACROSS), "mp")
    x_mid = x_in + mods[2] * attn
    unit2, inv2 = normalize(x_mid)
    h_mid = gather_rows((unit2 * (1.0 + mods[4]) + mods[3]).astype(LOW), "mp")
    upper = dot(h_mid, fc1_b)
    act_b = jax.nn.gelu(upper, approximate=False).astype(LOW)
    mlp = scatter_sum(dot(act_b, fc2_b, ACROSS), "mp")
    x_out = x_mid + mods[5] * mlp
    unit3, inv3 = normalize(x_out)
    h_fin = (unit3 * (1.0 + mods[7]) + mods[6]).astype(LOW)
    pred = dot(h_fin, head_b)
    diff = pred - noi
    loss_part = weight_tok * jnp.sum(diff * diff)

    d_pred = (2.0 * diff * (weight_tok / weight_total)).astype(LOW)
    d_head = dot(h_fin, d_pred, DOWN)
    d_out, d_shiftf, d_scalef = norm_back(dot(d_pred, head_b, ACROSS), unit3, inv3, mods[7])
    d_gate2 = jnp.sum(d_out * mlp, 0)
    d_mlp = gather_rows((d_out * mods[5]).astype(LOW), "mp")
    d_fc2 = dot(d_mlp, act_b, DOWN)
    d_act = dot(d_mlp, fc2_b)
    _, gelu_back = jax.vjp(lambda v: jax.nn.gelu(v, approximate=False), upper)
    d_upper = gelu_back(d_act)[0].astype(LOW)
    d_fc1 = dot(h_mid, d_upper, DOWN)
    d_hmid = scatter_sum(dot(d_upper, fc1_b, ACROSS), "mp")
    dx_mid, d_shift2, d_scale2 = norm_back(d_hmid, unit2, inv2, mods[4])
    d_mid = d_out + dx_mid
    d_gate1 = jnp.sum(d_mid * attn, 0)
    d_attn = gather_rows((d_mid * mods[2]).astype(LOW), "mp")
    d_outw = dot(d_attn, mixed_b, DOWN)
    d_mixed = heads_of(dot(d_attn, out_b).astype(LOW))
    d_query, d_key, d_value = attend_back(query, key, value, segment_ids, totals, d_mixed)
    d_qkv = jnp.concatenate([rows_of(g.astype(LOW)) for g in (d_query, d_key, d_value)], 1)
    d_wqkv = dot(h_in, d_qkv, DOWN)
    d_hin = scatter_sum(dot(d_qkv, qkv_b, ACROSS), "mp")
    dx_in, d_shift1, d_scale1 = norm_back(d_hin, unit1, inv1, mods[1])
    d_x = (d_mid + dx_in).astype(LOW)
    d_patch = dot(d_x, noisy_b, DOWN)

    sum_fc = scatter_sum(jnp.concatenate([d_fc1, d_fc2], 1), "dp")
    sum_at = scatter_sum(jnp.concatenate([d_wqkv, d_outw], 1), "dp")
    all_fc = gather_rows(sum_fc.astype(LOW), "dp")
    all_at = gather_rows(sum_at.astype(LOW), "dp")

    d_mods = jnp.stack([d_shift1, d_scale1, d_gate1, d_shift2, d_scale2, d_gate2, d_shiftf, d_scalef])
    blocks = exchange(d_mods.reshape(8, n_mp, width).transpose(1, 0, 2), "mp")
    first_only = (jnp.arange(SLOTS) == 0)[:, None, None]
    d_mod = jnp.where(single, jnp.where(first_only, jnp.sum(blocks, 0, keepdims=True), 0.0), blocks)
    d_mod = d_mod.astype(LOW).reshape(SLOTS, 8 * width)
    bundle = jnp.concatenate([d_mod, silu_c_b.reshape(SLOTS, -1)], 1)
    bundle = spread(bundle, "dp").reshape(n_dp, SLOTS, -1)
    d_mod_all = bundle[:, :, : 8 * width].reshape(slots_all, 8 * width)
    silu_c_all = (
        bundle[:, :, 8 * width :].reshape(n_dp, slots_all, rows).transpose(1, 0, 2).reshape(slots_all, -1)
    )
    g_mod_all = dot(silu_c_all, d_mod_all, DOWN)
    g_mod = dot(silu_c_b, d_mod_all, DOWN)
    d_cond_part = dot(d_mod_all, mod_b, ACROSS) * silu_slope(cond)
    d_silu_t_part = lax.dot_general(d_cond_part, time2_b.astype(F32), ALONG, precision=HIGH)
    thick = jnp.concatenate([d_silu_t_part.T, d_patch, d_head], 1)
    thick = jnp.sum(exchange(thick.reshape(n_dp, rows, -1), "dp"), 0)
    thick = lax.psum(jnp.concatenate([thick, d_cond_part.T], 1), "mp")
    d_silu_t = thick[:, :slots_all].T
    g_patch = thick[:, slots_all : slots_all + PIN]
    g_head = thick[:, slots_all + PIN : slots_all + 2 * PIN]
    d_cond = thick[:, slots_all + 2 * PIN :]
    g_table = lax.dot_general(d_cond, onehot, ALONG, precision=HIGH)
    g_time2 = lax.dot_general(d_cond, silu_t_b.astype(F32), ALONG, precision=HIGH)
    d_hidden = d_silu_t * silu_slope(hidden_t)
    g_time1 = lax.dot_general(d_hidden, feat_b.astype(F32), DOWN, precision=HIGH)
    g_cond = jnp.concatenate([g_patch, g_time1, g_time2, g_table], 1)

    square = lambda g: jnp.sum(g * g)
    split_sq = square(sum_fc) + square(sum_at) + square(g_mod)
    shared = lax.psum(jnp.stack([split_sq, loss_part]), "mp")
    tally = jnp.stack([shared[0] + square(g_head) + square(g_cond), shared[1]])
    tally = jnp.sum(spread(jnp.broadcast_to(tally[:, None], (2, 128)), "dp"), 0)
    grad_norm = jnp.sqrt(tally[0, 0])
    loss_sum = tally[1, 0]
    coef = jnp.minimum(1.0, CLIP / (grad_norm + 1e-06))

    moms = [m.reshape(rows, -1) for m in (mom_qkv, mom_out, mom_fc1, mom_fc2, mom_mod)]
    old = lax.all_gather(jnp.concatenate(moms, 1).astype(LOW), "dp", axis=0, tiled=True)
    masters = (w_qkv, w_out, w_fc1, w_fc2, w_mod)
    fresh = (
        sum_at[:, : 3 * width],
        sum_at[:, 3 * width :],
        sum_fc[:, :hidden],
        sum_fc[:, hidden:],
        g_mod,
    )
    whole = (all_at[:, : 3 * width], all_at[:, 3 * width :], all_fc[:, :hidden], all_fc[:, hidden:], g_mod_all)
    new_weights, new_moms = [], []
    start = 0
    for master, mom, grad, full in zip(masters, moms, fresh, whole):
        cols = mom.shape[1]
        new_moms.append((MU * mom + coef * grad).reshape(master.shape))
        full_mom = MU * old[:, start : start + cols].astype(F32) + coef * full.astype(F32)
        scale = 0.2 * math.sqrt(max(full_mom.shape))
        mine = (scale * orthogonal_rows(full_mom, me * rows, rows)).reshape(master.shape)
        new_weights.append(master * (1.0 - LR_MUON * DECAY) - LR_MUON * mine)
        start += cols

    adam_out = []
    for master, first, second, grad in (
        (w_head, first_head, second_head, g_head),
        (w_cond, first_cond, second_cond, g_cond),
    ):
        clipped = coef * grad
        first = BETA_ONE * first + (1.0 - BETA_ONE) * clipped
        second = BETA_TWO * second + (1.0 - BETA_TWO) * clipped * clipped
        update = first / (1.0 - BETA_ONE**STEP) / (jnp.sqrt(second / (1.0 - BETA_TWO**STEP)) + EPS_ADAM)
        adam_out.append((master - LR_ADAM * (update + DECAY * master), first, second))
    return (
        *new_weights,
        adam_out[0][0],
        adam_out[1][0],
        *new_moms,
        adam_out[0][1],
        adam_out[0][2],
        adam_out[1][1],
        adam_out[1][2],
        loss_sum,
        weight_total,
        grad_norm,
    )


def solution(mesh):
    row, wide, cube = P("dp", None), P("dp", "mp"), P("dp", None, "mp")
    in_specs = (
        *(row, row, P("dp"), row, row),
        *(cube, wide, wide, wide, cube, row, row),
        *(cube, wide, wide, wide, cube),
        *(row, row, row, row),
    )
    out_specs = (
        *(cube, wide, wide, wide, cube, row, row),
        *(cube, wide, wide, wide, cube),
        *(row, row, row, row),
        *(P(), P(), P()),
    )
    return jax.shard_map(body, mesh=mesh, in_specs=in_specs, out_specs=out_specs, check_vma=False)
```

time: 1950 us -> 907 us (0.47)
  waiting for transfers between devices: 1250 us -> 240 us
  blocking collectives: 227 us -> 23.9 us
  matrix products: 261 us -> 359 us
  starting transfers between devices: 1.17 us -> 53.5 us
  other arithmetic: 67.8 us -> 108 us
  loops' own time: 32.1 us -> 0 us
    reduce_scatter x8 -> x0, waiting for transfers between devices: 639 us -> none  [the longest x1 118 us: body(): lax.psum_scatter(d_condw, 'dp', scatter_dimension=0, tiled=True)]
    all_gather x8 -> x1, waiting for transfers between devices: 231 us -> 6.92 us  [body(): lax.all_gather(jnp.concatenate(moms, 1).astype(LOW), 'dp', axis=0, tiled=...]
    ppermute x0 -> x34, waiting for transfers between devices: none -> 202 us  [swap(): return lax.ppermute(x, axis, [(i, i ^ bit) for i in range(size)])]
    unnamed x28 -> x1, waiting for transfers between devices: 190 us -> 0.02 us
    psum x4 -> x0, waiting for transfers between devices: 189 us -> none  [the longest x1 65 us: layer_backward(): lax.psum(lax.dot_general(d_upper, fc1_b, ACROSS, preferred_element_type=j...]
    all_gather x4 -> x0, blocking collectives: 141 us -> none  [the longest x1 43.7 us: body(): lax.all_gather(w_qkv.astype(low_type), 'dp', axis=0, tiled=True)]
    dot_general x64 -> x84, matrix products: 257 us -> 359 us  [the longest x74 293 us: dot(): return lax.dot_general(a, b, dims, preferred_element_type=F32)]
    psum x3 -> x1, blocking collectives: 72.3 us -> 10.8 us  [body(): shared = lax.psum(jnp.stack([split_sq, loss_part]), 'mp')]
  transfers between devices with their start and end apart: 24 -> 42, of which waited for: 22 -> 30; matrix products, arithmetic and copies ran while one was open for 12% -> 24% of each run, Pallas kernels for 0% -> 0%
where the time goes in v1:
time: 907 us; the launch traced here: 900 us
  matrix products  359 us (40%)
  waiting for transfers between devices  240 us (26%)
  other arithmetic  108 us (12%)
  local copies, waits for them, and re-layouts  81.7 us (9%)
  starting transfers between devices  53.5 us (6%)
  between operations  34 us (4%)
  blocking collectives  23.9 us (3%)
    dot_general x74, matrix products, dot(): return lax.dot_general(a, b, dims, preferred_element_type=F32)  293 us
    ppermute x34, waiting for transfers between devices, swap(): return lax.ppermute(x, axis, [(i, i ^ bit) for i in range(size)])  202 us
    add x1, other arithmetic, body(): h_fin = (unit3 * (1.0 + mods[7]) + mods[6]).astype(LOW)  24.3 us
    ppermute x34, starting transfers between devices, swap(): return lax.ppermute(x, axis, [(i, i ^ bit) for i in range(size)])  24.2 us
    select_n x28, other arithmetic, gather_rows(): jnp.where(low_half, jnp.stack([cur, other], 1), jnp.stack([other, cur], 1))  22.7 us
    unnamed x271, local copies, waits for them, and re-layouts  22.3 us
    dot_general x1, matrix products, attend_back(): jnp.einsum('hqk,hkd->hqd', d_score, key, preferred_element_type=F32)  21.2 us
    dot_general x1, matrix products, attend_back(): jnp.einsum('hqk,hqd->hkd', d_score, query, preferred_element_type=F32)  21 us
  transfers between devices with their start and end apart: 42, of which 30 were waited for; matrix products, arithmetic and copies ran while one was open for 24% of the time, Pallas kernels for 0%

profile of v1, /device:TPU:0, one launch (start us, length us, event | category | flops | bytes accessed | tf_op | source)
XLA Modules:
  0.0 900.0 jit_solution(1761306962710111930)
XLA Ops:
  71.6 13.1 %all_gather.7 = f32[4,8,768]{1,0,2:T(4,128)S(1)} all-gather(f32[4,8,192]{1,0,2:T(4,128)S(1)} %copy.480), channel_id=1, replica_groups=mesh['dp'=8,'mp'=4] {'mp'}, dimensions={2}, use_global_device_ids=true | all-gather | bytes 122880 | tf_op jit(solution)/shard_map/all_gather | solution.py:272
  84.7 24.3 %fusion.286 = (f32[768]{0:T(1024)}, f32[768]{0:T(1024)}, f32[768]{0:T(1024)}, f32[768]{0:T(1024)S(1)}, f32[768]{0:T(1024)S(1)}, /*index=5*/f32[768]{0:T(1024)S(1)}, f32[768]{0:T(1024)}, f32[768]{0:T(1024)}) fusion(f32[4,8,768]{1,0,2:T(4,128)S(1)} %all_gather.7, s32[]{:T(128)S(6)} %select_n.619, s32[]{:T(128)S(6)} %add.743, s32[]{:T(128)S(6)} %add.742, ...), kind=kLoop, calls=%fused_computation.402 | loop fusion | flops 2304 | bytes 49184 | tf_op jit(solution)/shard_map/add | solution.py:299
  150.9 13.2 %collective-permute-done.7 = bf16[4,96,1728]{2,1,0:T(8,128)(2,1)} collective-permute-done((bf16[4,96,1728]{2,1,0:T(8,128)(2,1)}, bf16[4,96,1728]{2,1,0:T(8,128)(2,1)}, u32[]{:S(2)}, u32[]{:S(2)}) %collective-permute-start.7) | collective-permute-done | bytes 1327136 | tf_op jit(solution)/shard_map/ppermute | solution.py:42
  175.7 9.7 %collective-permute-done.9 = bf16[1,256,768]{2,1,0:T(8,128)(2,1)S(1)} collective-permute-done((bf16[1,256,768]{2,1,0:T(8,128)(2,1)S(1)}, bf16[1,256,768]{2,1,0:T(8,128)(2,1)S(1)}, u32[]{:S(2)}, u32[]{:S(2)}) %collective-permute-start.9) | collective-permute-done | bytes 393248 | tf_op jit(solution)/shard_map/ppermute | solution.py:42
  189.0 8.8 collective-permute-done.10
  203.0 9.6 %multiply_convert_fusion.1 = (bf16[1024,768]{1,0:T(8,128)(2,1)S(1)}, f32[1024,768]{1,0:T(8,128)}, f32[1024,768]{1,0:T(8,128)}) fusion(bf16[1024,768]{1,0:T(8,128)(2,1)S(1)} %bitcast.372, bf16[768,1728]{1,0:T(8,128)(2,1)S(1)} %bitcast.353), kind=kOutput, calls=%fused_computation.41 | convolution fusion | flops 1259077632 | bytes 10616832 | tf_op jit(solution)/shard_map/dot_general | solution.py:37
  235.5 8.8 collective-permute-done.14
  294.3 11.4 %collective-permute-done.16 = bf16[4,96,1536]{2,1,0:T(8,128)(2,1)} collective-permute-done((bf16[4,96,1536]{2,1,0:T(8,128)(2,1)}, bf16[4,96,1536]{2,1,0:T(8,128)(2,1)}, u32[]{:S(2)}, u32[]{:S(2)}) %collective-permute-start.16) | collective-permute-done | bytes 1179680 | tf_op jit(solution)/shard_map/ppermute | solution.py:42
  328.0 21.0 %fusion.52 = bf16[3,1024,64]{1,2,0:T(8,128)(2,1)} fusion(bf16[3,1024,64]{1,2,0:T(8,128)(2,1)} %bitcast.385, f32[3,1024,1024]{1,2,0:T(8,128)} %fusion.543, f32[3,1024,1024]{1,2,0:T(8,128)} %copy-done, f32[3,1024]{1,0:T(4,128)S(1)} %copy-done.112, pred[1024,1024]{0,1:T(8,128)(4,1)S(1)} %copy-done.5), kind=kOutput, calls=%fused_computation.142 | convolution fusion | flops 437456896 | bytes 27013120 | tf_op jit(solution)/shard_map/hqk,hqd->hkd/dot_general | solution.py:170
  349.0 21.2 %fusion.49 = bf16[3,1024,64]{1,2,0:T(8,128)(2,1)} fusion(bf16[3,1024,64]{1,2,0:T(8,128)(2,1)} %bitcast.383, f32[3,1024,1024]{1,2,0:T(8,128)} %fusion.543, f32[3,1024,1024]{1,2,0:T(8,128)} %copy-done, f32[3,1024]{1,0:T(4,128)S(1)} %copy-done.112, pred[1024,1024]{0,1:T(8,128)(4,1)S(1)} %copy-done.5), kind=kOutput, calls=%fused_computation.141 | convolution fusion | flops 437456896 | bytes 27013120 | tf_op jit(solution)/shard_map/hqk,hkd->hqd/dot_general | solution.py:169
  393.3 11.5 %collective-permute-done.24 = bf16[2,96,768]{2,1,0:T(8,128)(2,1)S(1)} collective-permute-done((bf16[2,96,768]{2,1,0:T(8,128)(2,1)S(1)}, bf16[2,96,768]{2,1,0:T(8,128)(2,1)S(1)}, u32[]{:S(2)}, u32[]{:S(2)}) %collective-permute-start.24) | collective-permute-done | bytes 294944 | tf_op jit(solution)/shard_map/ppermute | solution.py:42
  452.3 10.8 %all-reduce.1 = (f32[2]{0:T(128)S(1)}, f32[96,96]{0,1:T(8,128)S(1)}) all-reduce(f32[2]{0:T(128)S(1)} %pad_maximum_fusion.10, f32[96,96]{0,1:T(8,128)S(1)} %pad_maximum_fusion.3), channel_id=1, replica_groups=mesh['dp'=8,'mp'=4] {'mp'}, use_global_device_ids=true, to_apply=%region_32.33 | all-reduce | flops 9218 | bytes 73744 | tf_op jit(solution)/shard_map/psum | solution.py:364
  487.6 30.1 %collective-permute-done.31 = bf16[1,96,1536]{2,1,0:T(8,128)(2,1)S(1)} collective-permute-done((bf16[1,96,1536]{2,1,0:T(8,128)(2,1)S(1)}, bf16[1,96,1536]{2,1,0:T(8,128)(2,1)S(1)}, u32[]{:S(2)}, u32[]{:S(2)}) %collective-permute-start.31) | collective-permute-done | bytes 294944 | tf_op jit(solution)/shard_map/ppermute | solution.py:42
  518.0 19.2 %collective-permute-done.32 = bf16[2,96,1536]{2,1,0:T(8,128)(2,1)S(1)} collective-permute-done((bf16[2,96,1536]{2,1,0:T(8,128)(2,1)S(1)}, bf16[2,96,1536]{2,1,0:T(8,128)(2,1)S(1)}, u32[]{:S(2)}, u32[]{:S(2)}) %collective-permute-start.32) | collective-permute-done | bytes 589856 | tf_op jit(solution)/shard_map/ppermute | solution.py:42
  539.1 18.8 %collective-permute-done.28 = bf16[1,96,768]{2,1,0:T(8,128)(2,1)S(1)} collective-permute-done((bf16[1,96,768]{2,1,0:T(8,128)(2,1)S(1)}, bf16[1,96,768]{2,1,0:T(8,128)(2,1)S(1)}, u32[]{:S(2)}, u32[]{:S(2)}) %collective-permute-start.28) | collective-permute-done | bytes 147488 | tf_op jit(solution)/shard_map/ppermute | solution.py:42
  565.8 10.9 %collective-permute-done.29 = bf16[2,96,768]{2,1,0:T(8,128)(2,1)} collective-permute-done((bf16[2,96,768]{2,1,0:T(8,128)(2,1)}, bf16[2,96,768]{2,1,0:T(8,128)(2,1)}, u32[]{:S(2)}, u32[]{:S(2)}) %collective-permute-start.29) | collective-permute-done | bytes 294944 | tf_op jit(solution)/shard_map/ppermute | solution.py:42
  580.4 11.4 %collective-permute-done.33 = bf16[4,96,1536]{2,1,0:T(8,128)(2,1)} collective-permute-done((bf16[4,96,1536]{2,1,0:T(8,128)(2,1)S(1)}, bf16[4,96,1536]{2,1,0:T(8,128)(2,1)}, u32[]{:S(2)}, u32[]{:S(2)}) %collective-permute-start.33) | collective-permute-done | bytes 1179680 | tf_op jit(solution)/shard_map/ppermute | solution.py:42
  715.1 8.4 multiply_add_fusion.12
  728.8 8.3 multiply_add_fusion.11
  742.1 8.4 multiply_add_fusion.10
  826.0 9.2 %multiply_add_fusion.3 = f32[768,1536]{1,0:T(8,128)} fusion(f32[768,1536]{1,0:T(8,128)} %get-tuple-element.248, f32[]{:T(128)S(6)} %add.702, f32[768,768]{1,0:T(8,128)S(1)} %fusion.211), kind=kOutput, calls=%fused_computation.30 | convolution fusion | flops 2726756352 | bytes 11796484 | tf_op jit(solution)/shard_map/dot_general | solution.py:37
  841.0 8.4 multiply_add_fusion.2
  855.3 8.4 multiply_add_fusion.1
  869.5 8.4 multiply_add_fusion
  (658 shorter events, 552.4 us)
Async XLA Ops:
  12.4 32.2 %all-to-all-start = ((f32[8,104,32]{1,2,0:T(8,128)}), f32[8,104,32]{1,2,0:T(8,128)S(1)}, u32[]{:S(2)}, u32[]{:S(2)}) async-start(f32[8,104,32]{1,2,0:T(8,128)} %broadcast_in_dim.99), calls=%async_computation | async-start | bytes 262144 | tf_op jit(solution)/shard_map/all_to_all | solution.py:77
  20.8 19.9 %collective-permute-start.2 = (bf16[1,96,576]{1,2,0:T(8,128)(2,1)S(1)}, bf16[1,96,576]{1,2,0:T(8,128)(2,1)}, u32[]{:S(2)}, u32[]{:S(2)}) collective-permute-start(bf16[1,96,576]{1,2,0:T(8,128)(2,1)S(1)} %bitcast.387), channel_id=1, source_target_pairs={{0,16},{4,20},{8,24},{12,28},{16,0},{20,4},{24,8},{28,12},{1,17},{... | collective-permute-start | bytes 331784 | tf_op jit(solution)/shard_map/ppermute | solution.py:42
  26.1 83.8 %collective-permute-start.5 = (bf16[1,96,1728]{2,1,0:T(8,128)(2,1)S(1)}, bf16[1,96,1728]{2,1,0:T(8,128)(2,1)S(1)}, u32[]{:S(2)}, u32[]{:S(2)}) collective-permute-start(bf16[1,96,1728]{2,1,0:T(8,128)(2,1)S(1)} %concatenate.254), channel_id=1, source_target_pairs={{0,16},{4,20},{8,24},{12,28},{16,0},{20,4},{24,8},{28,12},{1,17},{... | collective-permute-start | bytes 995336 | tf_op jit(solution)/shard_map/ppermute | solution.py:42
  42.6 68.2 %collective-permute-start.3 = (bf16[2,96,576]{1,2,0:T(8,128)(2,1)}, bf16[2,96,576]{1,2,0:T(8,128)(2,1)}, u32[]{:S(2)}, u32[]{:S(2)}) collective-permute-start(bf16[2,96,576]{1,2,0:T(8,128)(2,1)} %maximum_select_fusion.23), channel_id=1, source_target_pairs={{0,8},{4,12},{8,0},{12,4},{16,24},{20,28},{24,16},{28,20},{1,9},{5... | collective-permute-start | bytes 663560 | tf_op jit(solution)/shard_map/ppermute | solution.py:42
  110.8 18.7 %collective-permute-start.6 = (bf16[2,96,1728]{2,1,0:T(8,128)(2,1)}, bf16[2,96,1728]{2,1,0:T(8,128)(2,1)}, u32[]{:S(2)}, u32[]{:S(2)}) collective-permute-start(bf16[2,96,1728]{2,1,0:T(8,128)(2,1)} %maximum_select_fusion.17), channel_id=1, source_target_pairs={{0,8},{4,12},{8,0},{12,4},{16,24},{20,28},{24,16},{28,20},{1,9},{5... | collective-permute-start | bytes 1990664 | tf_op jit(solution)/shard_map/ppermute | solution.py:42
  114.5 13.5 %collective-permute-start.4 = (bf16[4,96,576]{2,1,0:T(8,128)(2,1)}, bf16[4,96,576]{2,1,0:T(8,128)(2,1)}, u32[]{:S(2)}, u32[]{:S(2)}) collective-permute-start(bf16[4,96,576]{2,1,0:T(8,128)(2,1)} %copy.491), channel_id=1, source_target_pairs={{0,4},{4,0},{8,12},{12,8},{16,20},{20,16},{24,28},{28,24},{1,5},{5... | collective-permute-start | bytes 1327112 | tf_op jit(solution)/shard_map/ppermute | solution.py:42
  120.8 12.9 %collective-permute-start.1 = (bf16[2,256,768]{2,1,0:T(8,128)(2,1)S(1)}, bf16[2,256,768]{2,1,0:T(8,128)(2,1)S(1)}, u32[]{:S(2)}, u32[]{:S(2)}) collective-permute-start(bf16[2,256,768]{2,1,0:T(8,128)(2,1)S(1)} %maximum_select_fusion.11), channel_id=1, source_target_pairs={{0,1},{1,0},{2,3},{3,2},{4,5},{5,4},{6,7},{7,6},{8,9},{9,8},{10,11... | collective-permute-start | bytes 2359304 | tf_op jit(solution)/shard_map/ppermute | solution.py:42
  132.5 31.6 %collective-permute-start.7 = (bf16[4,96,1728]{2,1,0:T(8,128)(2,1)}, bf16[4,96,1728]{2,1,0:T(8,128)(2,1)}, u32[]{:S(2)}, u32[]{:S(2)}) collective-permute-start(bf16[4,96,1728]{2,1,0:T(8,128)(2,1)} %bitcast.47), channel_id=1, source_target_pairs={{0,4},{4,0},{8,12},{12,8},{16,20},{20,16},{24,28},{28,24},{1,5},{5... | collective-permute-start | bytes 3981320 | tf_op jit(solution)/shard_map/ppermute | solution.py:42
  264.4 13.9 %collective-permute-start.20 = (bf16[1,256,768]{2,1,0:T(8,128)(2,1)}, bf16[1,256,768]{2,1,0:T(8,128)(2,1)}, u32[]{:S(2)}, u32[]{:S(2)}) collective-permute-start(bf16[1,256,768]{2,1,0:T(8,128)(2,1)} %dynamic-slice_convert_fusion.4), channel_id=1, source_target_pairs={{0,2},{1,3},{2,0},{3,1},{4,6},{5,7},{6,4},{7,5},{8,10},{9,11},{10,... | collective-permute-start | bytes 1179656 | tf_op jit(solution)/shard_map/ppermute | solution.py:42
  277.5 28.3 %collective-permute-start.16 = (bf16[4,96,1536]{2,1,0:T(8,128)(2,1)}, bf16[4,96,1536]{2,1,0:T(8,128)(2,1)}, u32[]{:S(2)}, u32[]{:S(2)}) collective-permute-start(bf16[4,96,1536]{2,1,0:T(8,128)(2,1)} %fusion.64), channel_id=1, source_target_pairs={{0,4},{4,0},{8,12},{12,8},{16,20},{20,16},{24,28},{28,24},{1,5},{5... | collective-permute-start | bytes 3538952 | tf_op jit(solution)/shard_map/ppermute | solution.py:42
  294.2 17.9 %collective-permute-start.22 = (bf16[2,256,768]{2,1,0:T(8,128)(2,1)S(1)}, bf16[2,256,768]{2,1,0:T(8,128)(2,1)S(1)}, u32[]{:S(2)}, u32[]{:S(2)}) collective-permute-start(bf16[2,256,768]{2,1,0:T(8,128)(2,1)S(1)} %maximum_select_fusion.15), channel_id=1, source_target_pairs={{0,1},{1,0},{2,3},{3,2},{4,5},{5,4},{6,7},{7,6},{8,9},{9,8},{10,11... | collective-permute-start | bytes 2359304 | tf_op jit(solution)/shard_map/ppermute | solution.py:42
  310.4 76.2 %collective-permute-start.17 = (bf16[2,96,1536]{2,1,0:T(8,128)(2,1)}, bf16[2,96,1536]{2,1,0:T(8,128)(2,1)}, u32[]{:S(2)}, u32[]{:S(2)}) collective-permute-start(bf16[2,96,1536]{2,1,0:T(8,128)(2,1)} %fusion.239), channel_id=1, source_target_pairs={{0,8},{4,12},{8,0},{12,4},{16,24},{20,28},{24,16},{28,20},{1,9},{5... | collective-permute-start | bytes 1769480 | tf_op jit(solution)/shard_map/ppermute | solution.py:42
  377.4 14.3 %collective-permute-start.23 = (bf16[4,96,768]{2,1,0:T(8,128)(2,1)S(1)}, bf16[4,96,768]{2,1,0:T(8,128)(2,1)S(1)}, u32[]{:S(2)}, u32[]{:S(2)}) collective-permute-start(bf16[4,96,768]{2,1,0:T(8,128)(2,1)S(1)} %fusion.240), channel_id=1, source_target_pairs={{0,4},{4,0},{8,12},{12,8},{16,20},{20,16},{24,28},{28,24},{1,5},{5... | collective-permute-start | bytes 1769480 | tf_op jit(solution)/shard_map/ppermute | solution.py:42
  388.0 17.6 %collective-permute-start.18 = (bf16[1,96,1536]{2,1,0:T(8,128)(2,1)S(1)}, bf16[1,96,1536]{2,1,0:T(8,128)(2,1)S(1)}, u32[]{:S(2)}, u32[]{:S(2)}) collective-permute-start(bf16[1,96,1536]{2,1,0:T(8,128)(2,1)S(1)} %dynamic-slice_convert_fusion.8), channel_id=1, source_target_pairs={{0,16},{4,20},{8,24},{12,28},{16,0},{20,4},{24,8},{28,12},{1,17},{... | collective-permute-start | bytes 884744 | tf_op jit(solution)/shard_map/ppermute | solution.py:42
  391.8 13.0 %collective-permute-start.24 = (bf16[2,96,768]{2,1,0:T(8,128)(2,1)S(1)}, bf16[2,96,768]{2,1,0:T(8,128)(2,1)S(1)}, u32[]{:S(2)}, u32[]{:S(2)}) collective-permute-start(bf16[2,96,768]{2,1,0:T(8,128)(2,1)S(1)} %fusion.292), channel_id=1, source_target_pairs={{0,8},{4,12},{8,0},{12,4},{16,24},{20,28},{24,16},{28,20},{1,9},{5... | collective-permute-start | bytes 884744 | tf_op jit(solution)/shard_map/ppermute | solution.py:42
  392.7 21.6 %collective-permute-start.27 = (bf16[1,256,768]{2,1,0:T(8,128)(2,1)S(1)}, bf16[1,256,768]{2,1,0:T(8,128)(2,1)S(1)}, u32[]{:S(2)}, u32[]{:S(2)}) collective-permute-start(bf16[1,256,768]{2,1,0:T(8,128)(2,1)S(1)} %dynamic-slice_convert_fusion.3), channel_id=1, source_target_pairs={{0,2},{1,3},{2,0},{3,1},{4,6},{5,7},{6,4},{7,5},{8,10},{9,11},{10,... | collective-permute-start | bytes 1179656 | tf_op jit(solution)/shard_map/ppermute | solution.py:42
  439.4 11.9 %all-to-all-start.5 = ((f32[8,96,64]{1,2,0:T(8,128)}), f32[8,96,64]{1,2,0:T(8,128)S(1)}, u32[]{:S(2)}, u32[]{:S(2)}) async-start(f32[8,96,64]{1,2,0:T(8,128)} %copy.517), calls=%async_computation.5 | async-start | bytes 524288 | tf_op jit(solution)/shard_map/all_to_all | solution.py:81
  473.3 146.7 %all-gather.2.cloned.1.call-start = ((), (), s32[]{:S(2)}) async-start(), calls=%async_computation.7 | async-start | bytes 6635520 | tf_op jit(solution)/shard_map/all_gather | solution.py:372
  487.0 30.7 %collective-permute-start.31 = (bf16[1,96,1536]{2,1,0:T(8,128)(2,1)S(1)}, bf16[1,96,1536]{2,1,0:T(8,128)(2,1)S(1)}, u32[]{:S(2)}, u32[]{:S(2)}) collective-permute-start(bf16[1,96,1536]{2,1,0:T(8,128)(2,1)S(1)} %fusion.288), channel_id=1, source_target_pairs={{0,16},{4,20},{8,24},{12,28},{16,0},{20,4},{24,8},{28,12},{1,17},{... | collective-permute-start | bytes 884744 | tf_op jit(solution)/shard_map/ppermute | solution.py:42
  517.8 19.4 %collective-permute-start.32 = (bf16[2,96,1536]{2,1,0:T(8,128)(2,1)S(1)}, bf16[2,96,1536]{2,1,0:T(8,128)(2,1)S(1)}, u32[]{:S(2)}, u32[]{:S(2)}) collective-permute-start(bf16[2,96,1536]{2,1,0:T(8,128)(2,1)S(1)} %maximum_select_fusion.21), channel_id=1, source_target_pairs={{0,8},{4,12},{8,0},{12,4},{16,24},{20,28},{24,16},{28,20},{1,9},{5... | collective-permute-start | bytes 1769480 | tf_op jit(solution)/shard_map/ppermute | solution.py:42
  537.6 54.2 %collective-permute-start.33 = (bf16[4,96,1536]{2,1,0:T(8,128)(2,1)S(1)}, bf16[4,96,1536]{2,1,0:T(8,128)(2,1)}, u32[]{:S(2)}, u32[]{:S(2)}) collective-permute-start(bf16[4,96,1536]{2,1,0:T(8,128)(2,1)S(1)} %bitcast.349), channel_id=1, source_target_pairs={{0,4},{4,0},{8,12},{12,8},{16,20},{20,16},{24,28},{28,24},{1,5},{5... | collective-permute-start | bytes 3538952 | tf_op jit(solution)/shard_map/ppermute | solution.py:42
  539.0 18.9 %collective-permute-start.28 = (bf16[1,96,768]{2,1,0:T(8,128)(2,1)S(1)}, bf16[1,96,768]{2,1,0:T(8,128)(2,1)S(1)}, u32[]{:S(2)}, u32[]{:S(2)}) collective-permute-start(bf16[1,96,768]{2,1,0:T(8,128)(2,1)S(1)} %fusion.313), channel_id=1, source_target_pairs={{0,16},{4,20},{8,24},{12,28},{16,0},{20,4},{24,8},{28,12},{1,17},{... | collective-permute-start | bytes 442376 | tf_op jit(solution)/shard_map/ppermute | solution.py:42
  558.7 18.0 %collective-permute-start.29 = (bf16[2,96,768]{2,1,0:T(8,128)(2,1)}, bf16[2,96,768]{2,1,0:T(8,128)(2,1)}, u32[]{:S(2)}, u32[]{:S(2)}) collective-permute-start(bf16[2,96,768]{2,1,0:T(8,128)(2,1)} %maximum_select_fusion.25), channel_id=1, source_target_pairs={{0,8},{4,12},{8,0},{12,4},{16,24},{20,28},{24,16},{28,20},{1,9},{5... | collective-permute-start | bytes 884744 | tf_op jit(solution)/shard_map/ppermute | solution.py:42
  578.9 28.0 %collective-permute-start.30 = (bf16[4,96,768]{2,1,0:T(8,128)(2,1)}, bf16[4,96,768]{2,1,0:T(8,128)(2,1)}, u32[]{:S(2)}, u32[]{:S(2)}) collective-permute-start(bf16[4,96,768]{2,1,0:T(8,128)(2,1)} %bitcast.129), channel_id=1, source_target_pairs={{0,4},{4,0},{8,12},{12,8},{16,20},{20,16},{24,28},{28,24},{1,5},{5... | collective-permute-start | bytes 1769480 | tf_op jit(solution)/shard_map/ppermute | solution.py:42
  (151 other events, 1513.2 us)
Sparse Core Ops, SparseCore 0:
  487.0 133.0 all-gather.1

commit v2 on v1

v2 whole, which is shorter than its diff:
```python
import functools
import math

import jax
import jax.numpy as jnp
from jax import lax
from jax.experimental import pallas as pl
from jax.experimental.pallas import tpu as pltpu
from jax.sharding import PartitionSpec as P

SIDE = 32
D = 768
HEAD_DIM = 64
CLASSES = 1001
FREQ = 256
PIN = 16
STEP = 10
SLOTS = 4

HIGH = lax.Precision.HIGHEST
GAMMA = 5.0
CLIP = 0.05
MU = 0.95
LR_MUON = 0.1
DECAY = 0.01
BETA_ONE = 0.9
BETA_TWO = 0.95
LR_ADAM = 0.08
EPS_ADAM = 1e-08
NS_COEF = (3.4445, -4.775, 2.0315)
NS_SHIFT = (0.0, 0.1, 0.5, 0.8, 0.8)
ACROSS = (((1,), (1,)), ((), ()))
DOWN = (((0,), (0,)), ((), ()))
ALONG = (((1,), (0,)), ((), ()))
LOW = jnp.bfloat16
F32 = jnp.float32


def dot(a, b, dims=ALONG):
    return lax.dot_general(a, b, dims, preferred_element_type=F32)


def swap(x, axis, bit):
    size = lax.axis_size(axis)
    return lax.ppermute(x, axis, [(i, i ^ bit) for i in range(size)])


def after(x, *others):
    return lax.optimization_barrier((x,) + others)[0]


def gather_steps(x, axis):
    size = lax.axis_size(axis)
    me = lax.axis_index(axis)
    cur = x[None]
    bit = size // 2
    while bit >= 1:
        other = swap(cur, axis, bit)
        other = yield other
        low_half = (me // bit) % 2 == 0
        cur = jnp.where(low_half, jnp.stack([cur, other], 1), jnp.stack([other, cur], 1))
        cur = cur.reshape((-1,) + x.shape)
        bit //= 2
    return cur.reshape((-1,) + x.shape[1:])


def sum_steps(x, axis):
    size = lax.axis_size(axis)
    me = lax.axis_index(axis)
    cur = x.reshape((size, x.shape[0] // size) + x.shape[1:])
    bit = 1
    while bit < size:
        pair = cur.reshape((cur.shape[0] // 2, 2) + cur.shape[1:])
        mine = (me // bit) % 2
        keep = lax.dynamic_index_in_dim(pair, mine, 1, keepdims=False)
        send = lax.dynamic_index_in_dim(pair, 1 - mine, 1, keepdims=False)
        other = swap(send.astype(LOW), axis, bit)
        other = yield other
        cur = keep.astype(F32) + other.astype(F32)
        bit *= 2
    return cur[0]


class Course:
    def __init__(self, steps):
        self.steps = steps
        self.result = None
        self.flight = next(steps)

    def step(self, x=None):
        arrived = self.flight
        if arrived is None:
            return x
        if x is not None:
            x = after(x, arrived)
        try:
            self.flight = self.steps.send(arrived)
        except StopIteration as stop:
            self.flight, self.result = None, stop.value
        return x

    def finish(self):
        while self.flight is not None:
            self.step()
        return self.result


def gather_rows(x, axis):
    return Course(gather_steps(x, axis)).finish()


def scatter_sum(x, axis):
    return Course(sum_steps(x, axis)).finish()


def sum_all(x, axis):
    bit = 1
    while bit < lax.axis_size(axis):
        x = x + swap(x, axis, bit)
        bit *= 2
    return x


def spread(x, axis):
    size = lax.axis_size(axis)
    copies = jnp.broadcast_to(x[None], (size,) + x.shape)
    return lax.all_to_all(copies, axis, 0, 0, tiled=True)


def exchange(x, axis):
    return lax.all_to_all(x, axis, 0, 0, tiled=True)


def plan():
    betas = jnp.linspace(0.0001, 0.02, 1000, dtype=F32)
    return jnp.cumprod(1.0 - betas)


def pick(table, index):
    grid = jnp.arange(table.shape[0], dtype=jnp.int32)
    return jnp.sum(jnp.where(index[..., None] == grid, table, 0.0), -1)


def normalize(x):
    cent = x - jnp.mean(x, -1, keepdims=True)
    inv = lax.rsqrt(jnp.mean(cent * cent, -1, keepdims=True) + 1e-06)
    return cent * inv, inv


def norm_back(grad, unit, inv, scale):
    d_shift = jnp.sum(grad, 0)
    d_scale = jnp.sum(grad * unit, 0)
    g = grad * (1.0 + scale)
    dx = inv * (g - jnp.mean(g, -1, keepdims=True) - unit * jnp.mean(g * unit, -1, keepdims=True))
    return dx, d_shift, d_scale


def place_table():
    quarter = D // 4
    column = jnp.arange(D, dtype=jnp.int32)
    omega = 1.0 / 10000.0 ** ((column % quarter).astype(F32) / quarter)
    angle = jnp.arange(SIDE, dtype=F32)[:, None] * omega
    wave = jnp.where((column // quarter) % 2 == 0, jnp.sin(angle), jnp.cos(angle))
    down = column < D // 2
    return jnp.concatenate([jnp.where(down, wave, 0.0), jnp.where(down, 0.0, wave)], 0)


def place_select(single, part, rank):
    local = jnp.arange(part, dtype=jnp.int32)
    full = rank * part + local
    half = SIDE // 2
    down = jnp.where(single, full // SIDE, local // half)
    across = jnp.where(single, full % SIDE, local % half)
    grid = jnp.arange(SIDE, dtype=jnp.int32)
    return jnp.concatenate([down[:, None] == grid, across[:, None] == grid], 1)


def thirds(x):
    high = x.astype(LOW)
    rest = x - high.astype(F32)
    mid = rest.astype(LOW)
    return high, mid, (rest - mid.astype(F32)).astype(LOW)


def time_features(steps):
    half = FREQ // 2
    freqs = jnp.exp(-math.log(10000.0) * jnp.arange(half, dtype=F32) / half)
    angles = steps.astype(F32)[:, None] * freqs
    return jnp.concatenate([jnp.cos(angles), jnp.sin(angles)], -1)


def silu_slope(x):
    s = jax.nn.sigmoid(x)
    return s * (1.0 + x * (1.0 - s))


def params():
    return pltpu.CompilerParams(vmem_limit_bytes=48 * 2**20)


def turned(x):
    return x.astype(F32).T.astype(x.dtype)


def attend_kernel(single_ref, qkv_ref, mixed_ref, total_ref, vt_ref):
    part, width = mixed_ref.shape
    i = pl.program_id(0)
    mine = pl.ds(pl.multiple_of(i * part, part), part)

    @pl.when(i == 0)
    def _():
        vt_ref[...] = turned(qkv_ref[:, 2 * width :])

    def run(keys):
        outs = []
        for h in range(width // HEAD_DIM):
            lo = h * HEAD_DIM
            q = qkv_ref[mine, lo : lo + HEAD_DIM] * HEAD_DIM**-0.5
            k = qkv_ref[keys, width + lo : width + lo + HEAD_DIM]
            s = dot(k, q, ACROSS)
            top = jnp.max(s, axis=0, keepdims=True)
            e = jnp.exp(s - top)
            z = jnp.sum(e, axis=0, keepdims=True)
            total_ref[h : h + 1, :] = top + jnp.log(z)
            outs.append(dot(vt_ref[lo : lo + HEAD_DIM, keys], (e * (1.0 / z)).astype(LOW)))
        mixed_ref[...] = jnp.concatenate(outs, 0).T.astype(LOW)

    @pl.when(single_ref[0] == 1)
    def _():
        run(slice(None))

    @pl.when(single_ref[0] != 1)
    def _():
        run(mine)


def attend(single, qkv, part):
    tokens, columns = qkv.shape
    width = columns // 3
    return pl.pallas_call(
        attend_kernel,
        grid=(tokens // part,),
        out_shape=(
            jax.ShapeDtypeStruct((tokens, width), LOW),
            jax.ShapeDtypeStruct((8, tokens), F32),
        ),
        in_specs=[
            pl.BlockSpec(memory_space=pltpu.SMEM),
            pl.BlockSpec((tokens, columns), lambda i: (0, 0)),
        ],
        out_specs=(
            pl.BlockSpec((part, width), lambda i: (i, 0)),
            pl.BlockSpec((8, part), lambda i: (0, i)),
        ),
        scratch_shapes=[pltpu.VMEM((width, tokens), LOW)],
        compiler_params=params(),
        cost_estimate=pl.CostEstimate(
            flops=4 * tokens * tokens * width,
            bytes_accessed=8 * tokens * width,
            transcendentals=tokens * tokens * width // HEAD_DIM,
        ),
        name="attend",
    )(single, qkv)


def attend_back_kernel(single_ref, qkv_ref, grad_ref, total_ref, out_ref, kt_ref, dk_ref, dv_ref):
    width = qkv_ref.shape[1] // 3
    part = grad_ref.shape[0]
    heads = width // HEAD_DIM
    i = pl.program_id(0)
    mine = pl.ds(pl.multiple_of(i * part, part), part)

    @pl.when(i == 0)
    def _():
        kt_ref[...] = turned(qkv_ref[:, width : 2 * width] * HEAD_DIM**-0.5)
        dk_ref[...] = jnp.zeros_like(dk_ref)
        dv_ref[...] = jnp.zeros_like(dv_ref)

    def run(keys):
        outs = []
        for h in range(heads):
            lo = h * HEAD_DIM
            q = qkv_ref[mine, lo : lo + HEAD_DIM] * HEAD_DIM**-0.5
            k = qkv_ref[keys, width + lo : width + lo + HEAD_DIM]
            v = qkv_ref[keys, 2 * width + lo : 2 * width + lo + HEAD_DIM]
            g = grad_ref[:, lo : lo + HEAD_DIM]
            p = jnp.exp(dot(k, q, ACROSS) - total_ref[h : h + 1, :])
            dp = dot(v, g, ACROSS)
            delta = jnp.sum(dp * p, axis=0, keepdims=True)
            ds = (p * (dp - delta)).astype(LOW)
            dv_ref[h, keys, :] += dot(p.astype(LOW), g)
            dk_ref[h, keys, :] += dot(ds, q)
            outs.append(dot(kt_ref[lo : lo + HEAD_DIM, keys], ds))
        out_ref[mine, :width] = jnp.concatenate(outs, 0).T.astype(LOW)

    @pl.when(single_ref[0] == 1)
    def _():
        run(slice(None))

    @pl.when(single_ref[0] != 1)
    def _():
        run(mine)

    @pl.when(i == pl.num_programs(0) - 1)
    def _():
        for h in range(heads):
            lo = h * HEAD_DIM
            out_ref[:, width + lo : width + lo + HEAD_DIM] = dk_ref[h].astype(LOW)
            out_ref[:, 2 * width + lo : 2 * width + lo + HEAD_DIM] = dv_ref[h].astype(LOW)


def attend_back(single, qkv, grad, totals, part):
    tokens, columns = qkv.shape
    width = columns // 3
    heads = width // HEAD_DIM
    return pl.pallas_call(
        attend_back_kernel,
        grid=(tokens // part,),
        out_shape=jax.ShapeDtypeStruct((tokens, columns), LOW),
        in_specs=[
            pl.BlockSpec(memory_space=pltpu.SMEM),
            pl.BlockSpec((tokens, columns), lambda i: (0, 0)),
            pl.BlockSpec((part, width), lambda i: (i, 0)),
            pl.BlockSpec((8, part), lambda i: (0, i)),
        ],
        out_specs=pl.BlockSpec((tokens, columns), lambda i: (0, 0)),
        scratch_shapes=[
            pltpu.VMEM((width, tokens), LOW),
            pltpu.VMEM((heads, tokens, HEAD_DIM), F32),
            pltpu.VMEM((heads, tokens, HEAD_DIM), F32),
        ],
        compiler_params=params(),
        cost_estimate=pl.CostEstimate(
            flops=10 * tokens * tokens * width,
            bytes_accessed=14 * tokens * width,
            transcendentals=tokens * tokens * heads,
        ),
        name="attend_back",
    )(single, qkv, grad, totals)


def muon_kernel(tile, columns, own_ref, coef_ref, mom_ref, *refs):
    grads, (out_ref, x_ref, a_ref, b_ref, e_ref, eb_ref) = refs[:-6], refs[-6:]
    first, second, third = NS_COEF
    size, count = x_ref.shape[0], out_ref.shape[0]
    tiles = size // tile
    coef = coef_ref[0]
    span = slice(*columns)

    def rows(i):
        return pl.ds(pl.multiple_of(i * tile, tile), tile)

    def load(i, total):
        if len(grads) == 2:
            grad = dot(grads[0][rows(i), :], grads[1][...])
        else:
            grad = grads[0][rows(i), span].astype(F32)
        x = MU * mom_ref[rows(i), span].astype(F32) + coef * grad
        x_ref[rows(i), :] = x
        return total + jnp.sum(x * x, axis=0, keepdims=True)

    squares = lax.fori_loop(0, tiles, load, jnp.zeros((1, x_ref.shape[1]), F32))
    inv = 1.0 / (jnp.sqrt(jnp.sum(squares, axis=1, keepdims=True)) + 1e-07)

    def scale(i, carry):
        x = x_ref[rows(i), :] * inv
        x_ref[rows(i), :] = x
        a_ref[rows(i), :] = x.astype(LOW)
        return carry

    lax.fori_loop(0, tiles, scale, 0)
    cur, new = a_ref, b_ref
    for turn, shift in enumerate(NS_SHIFT):
        centre = first + second * shift + third * shift * shift
        slope = second + 2.0 * third * shift

        def gram(i, carry):
            e = dot(cur[rows(i), :], cur[...], ACROSS)
            if shift:
                row = lax.broadcasted_iota(jnp.int32, e.shape, 0) + i * tile
                column = lax.broadcasted_iota(jnp.int32, e.shape, 1)
                e = e - jnp.where(row == column, shift, 0.0)
            e_ref[rows(i), :] = e
            eb_ref[rows(i), :] = e.astype(LOW)
            return carry

        def step(i, carry):
            poly = slope * e_ref[rows(i), :] + third * dot(eb_ref[rows(i), :], eb_ref[...])
            x = centre * x_ref[rows(i), :] + dot(poly.astype(LOW), cur[...])
            x_ref[rows(i), :] = x
            new[rows(i), :] = x.astype(LOW)
            return carry

        lax.fori_loop(0, tiles, gram, 0)
        if turn < len(NS_SHIFT) - 1:
            lax.fori_loop(0, tiles, step, 0)
            cur, new = new, cur
        else:
            own = pl.ds(pl.multiple_of(own_ref[0], 16), count)
            e = e_ref[own, :]
            poly = slope * e + third * dot(e.astype(LOW), eb_ref[...])
            x = centre * x_ref[own, :] + dot(poly.astype(LOW), cur[...])
            out_ref[...] = (0.2 * math.sqrt(max(x_ref.shape)) * x).astype(LOW)


def muon_rows(own, count, coef, mom, mom_block, grads, grad_block, block, columns):
    size = mom.shape[0]
    width = columns[1] - columns[0]
    tile = size // 2 if width > size else size
    whole = lambda a: pl.BlockSpec(a.shape, lambda i: (0, 0))
    packed = lambda k: pl.BlockSpec((size, block), lambda i: (0, k))
    smem = pl.BlockSpec(memory_space=pltpu.SMEM)
    return pl.pallas_call(
        functools.partial(muon_kernel, tile, columns),
        grid=(1,),
        out_shape=jax.ShapeDtypeStruct((count, width), LOW),
        in_specs=[smem, smem, packed(mom_block)]
        + ([whole(g) for g in grads] if len(grads) == 2 else [packed(grad_block)]),
        out_specs=pl.BlockSpec((count, width), lambda i: (0, 0)),
        scratch_shapes=[
            pltpu.VMEM((size, width), F32),
            pltpu.VMEM((size, width), LOW),
            pltpu.VMEM((size, width), LOW),
            pltpu.VMEM((size, size), F32),
            pltpu.VMEM((size, size), LOW),
        ],
        compiler_params=params(),
        cost_estimate=pl.CostEstimate(
            flops=10 * size * size * (2 * width + size), bytes_accessed=6 * size * width, transcendentals=0
        ),
        name="muon",
    )(own, coef, mom, *grads)


def body(
    latents,
    noise,
    segment_ids,
    timesteps,
    labels,
    w_qkv,
    w_out,
    w_fc1,
    w_fc2,
    w_mod,
    w_head,
    w_cond,
    mom_qkv,
    mom_out,
    mom_fc1,
    mom_fc2,
    mom_mod,
    first_head,
    second_head,
    first_cond,
    second_cond,
):
    n_dp, n_mp = lax.axis_size("dp"), lax.axis_size("mp")
    me, rank = lax.axis_index("dp"), lax.axis_index("mp")
    tokens = latents.shape[0]
    part = tokens // n_mp
    rows = w_qkv.shape[0]
    width = w_qkv.shape[2]
    hidden = w_fc1.shape[1]

    qkv_way = Course(gather_steps(w_qkv.reshape(rows, -1).astype(LOW), "dp"))
    rest_way = Course(gather_steps(jnp.concatenate([w_out, w_fc1, w_fc2], 1).astype(LOW), "dp"))

    single = jnp.max(segment_ids) == 0
    note = jnp.concatenate(
        [
            timesteps.reshape(-1).astype(F32),
            labels.reshape(-1).astype(F32),
            single.astype(F32)[None],
            jnp.zeros((2 * PIN - 2 * SLOTS - 1,), F32),
        ]
    )
    thin = jnp.concatenate([w_cond[:, :PIN], w_head], 1)
    packet = spread(jnp.concatenate([thin, jnp.broadcast_to(note, (8, 2 * PIN))], 0), "dp")
    packet = packet.reshape(n_dp, rows + 8, 2 * PIN)
    thin_b = packet[:, :rows].reshape(n_dp * rows, 2 * PIN).astype(LOW)
    patch_b, head_b = thin_b[:, :PIN], thin_b[:, PIN:]
    notes = packet[:, rows]
    steps = notes[:, :SLOTS].astype(jnp.int32)
    kinds = notes[:, SLOTS : 2 * SLOTS].astype(jnp.int32).reshape(-1)
    singles = notes[:, 2 * SLOTS] > 0.5

    abar = pick(plan(), steps)
    snr = abar / (1.0 - abar)
    slot_weight = jnp.minimum(snr, GAMMA) / snr
    weight_total = part * jnp.sum(jnp.where(singles[:, None], n_mp * slot_weight[:, :1] / SLOTS, slot_weight))

    time1_b = w_cond[:, PIN : PIN + FREQ].astype(LOW)
    time2_b = w_cond[:, PIN + FREQ : PIN + FREQ + D].astype(LOW)
    table_b = w_cond[:, PIN + FREQ + D :].astype(LOW)
    mod_b = w_mod.reshape(rows, -1).astype(LOW)
    feat_b = time_features(steps.reshape(-1)).astype(LOW)
    slots_all = feat_b.shape[0]
    hidden_t = dot(feat_b, time1_b, ACROSS)
    silu_own = qkv_way.step(jax.nn.silu(hidden_t).astype(LOW))
    silu_t = spread(silu_own, "dp").reshape(n_dp, slots_all, rows)
    silu_t_b = silu_t.transpose(1, 0, 2).reshape(slots_all, n_dp * rows)
    onehot = (kinds[:, None] == jnp.arange(CLASSES, dtype=jnp.int32)).astype(F32)
    cond = dot(silu_t_b, time2_b, ACROSS) + dot(onehot.astype(LOW), table_b, ACROSS)
    silu_c_b = jax.nn.silu(cond).astype(LOW)
    mod_part = rest_way.step(qkv_way.step(dot(silu_c_b, mod_b)))
    mod_cols = jnp.sum(exchange(mod_part.reshape(n_dp, SLOTS, -1), "dp"), 0).reshape(SLOTS, 8, width)
    mod_cols = rest_way.step(mod_cols)
    part_slots = segment_ids[::part]
    outgoing = jnp.sum(
        jnp.where((part_slots[:, None] == jnp.arange(SLOTS))[:, :, None, None], mod_cols[None], 0.0), 1
    )
    mods = exchange(outgoing, "mp").transpose(1, 0, 2).reshape(8, n_mp * width)
    slot = lax.dynamic_index_in_dim(part_slots, rank, 0, keepdims=False)

    my_row = lambda a: lax.dynamic_index_in_dim(a, me, 0, keepdims=False)
    my_slot = lambda a: lax.dynamic_index_in_dim(my_row(a), slot, 0, keepdims=False)
    abar_tok, weight_tok = my_slot(abar), my_slot(slot_weight)
    lat = lax.dynamic_slice_in_dim(latents, rank * part, part, 0)
    noi = lax.dynamic_slice_in_dim(noise, rank * part, part, 0)
    noisy_b = (jnp.sqrt(abar_tok) * lat + jnp.sqrt(1.0 - abar_tok) * noi).astype(LOW)
    picks = place_select(single, part, rank).astype(LOW)
    left = jnp.concatenate([noisy_b, picks, picks, picks], 1)
    x_in = dot(left, jnp.concatenate([patch_b.T, *thirds(place_table())], 0))
    unit1, inv1 = normalize(x_in)
    h_in = gather_rows((unit1 * (1.0 + mods[1]) + mods[0]).astype(LOW), "mp")

    alone = single.astype(jnp.int32)[None]
    qkv_b = qkv_way.finish()
    qkv = dot(h_in, qkv_b).astype(LOW)
    rest = rest_way.finish()
    out_b, fc1_b, fc2_b = rest[:, :width], rest[:, width : width + hidden], rest[:, width + hidden :]
    mixed_b, totals = attend(alone, after(qkv, rest), part)
    attn = scatter_sum(dot(mixed_b, out_b, ACROSS), "mp")
    x_mid = x_in + mods[2] * attn
    unit2, inv2 = normalize(x_mid)
    h_mid = gather_rows((unit2 * (1.0 + mods[4]) + mods[3]).astype(LOW), "mp")
    upper = dot(h_mid, fc1_b)
    act_b = jax.nn.gelu(upper, approximate=False).astype(LOW)
    mlp = scatter_sum(dot(act_b, fc2_b, ACROSS), "mp")
    x_out = x_mid + mods[5] * mlp
    unit3, inv3 = normalize(x_out)
    h_fin = (unit3 * (1.0 + mods[7]) + mods[6]).astype(LOW)
    pred = dot(h_fin, head_b)
    diff = pred - noi
    loss_part = weight_tok * jnp.sum(diff * diff)

    d_pred = (2.0 * diff * (weight_tok / weight_total)).astype(LOW)
    d_head = dot(h_fin, d_pred, DOWN)
    d_out, d_shiftf, d_scalef = norm_back(dot(d_pred, head_b, ACROSS), unit3, inv3, mods[7])
    d_gate2 = jnp.sum(d_out * mlp, 0)
    d_mlp = gather_rows((d_out * mods[5]).astype(LOW), "mp")
    moms = [m.reshape(rows, -1) for m in (mom_mod, mom_fc1, mom_fc2, mom_qkv, mom_out)]
    old = jnp.concatenate([m.astype(LOW) for m in moms], 1)
    old = lax.all_gather(after(old, mixed_b), "dp", axis=0, tiled=True)
    d_mlp = after(d_mlp, old)
    d_fc2 = dot(d_mlp, act_b, DOWN)
    d_act = dot(d_mlp, fc2_b)
    _, gelu_back = jax.vjp(lambda v: jax.nn.gelu(v, approximate=False), upper)
    d_upper = gelu_back(d_act)[0].astype(LOW)
    d_fc1 = dot(h_mid, d_upper, DOWN)
    fc_way = Course(sum_steps(jnp.concatenate([d_fc1, d_fc2], 1), "dp"))
    d_hmid = scatter_sum(dot(d_upper, fc1_b, ACROSS), "mp")
    dx_mid, d_shift2, d_scale2 = norm_back(d_hmid, unit2, inv2, mods[4])
    d_mid = d_out + dx_mid
    d_gate1 = jnp.sum(d_mid * attn, 0)
    d_attn = gather_rows((d_mid * mods[2]).astype(LOW), "mp")
    d_outw = dot(d_attn, mixed_b, DOWN)
    d_mixed = fc_way.step(dot(d_attn, out_b).astype(LOW))
    d_qkv = fc_way.step(attend_back(alone, qkv, d_mixed, totals, part))
    d_wqkv = dot(h_in, d_qkv, DOWN)
    at_way = Course(sum_steps(jnp.concatenate([d_wqkv, d_outw], 1), "dp"))
    d_hin = fc_way.step(scatter_sum(dot(d_qkv, qkv_b, ACROSS), "mp"))
    sum_fc = fc_way.finish()
    fc_way = Course(gather_steps(sum_fc.astype(LOW), "dp"))
    dx_in, d_shift1, d_scale1 = norm_back(d_hin, unit1, inv1, mods[1])
    d_x = (d_mid + dx_in).astype(LOW)
    d_patch = dot(d_x, noisy_b, DOWN)

    d_mods = jnp.stack([d_shift1, d_scale1, d_gate1, d_shift2, d_scale2, d_gate2, d_shiftf, d_scalef])
    blocks = exchange(d_mods.reshape(8, n_mp, width).transpose(1, 0, 2), "mp")
    first_only = (jnp.arange(SLOTS) == 0)[:, None, None]
    d_mod = jnp.where(single, jnp.where(first_only, jnp.sum(blocks, 0, keepdims=True), 0.0), blocks)
    d_mod = d_mod.astype(LOW).reshape(SLOTS, 8 * width)
    bundle = at_way.step(jnp.concatenate([d_mod, silu_c_b.reshape(SLOTS, -1)], 1))
    bundle = spread(bundle, "dp").reshape(n_dp, SLOTS, -1)
    d_mod_all = bundle[:, :, : 8 * width].reshape(slots_all, 8 * width)
    silu_c_all = (
        bundle[:, :, 8 * width :].reshape(n_dp, slots_all, rows).transpose(0, 2, 1).reshape(-1, slots_all)
    )
    g_mod = dot(silu_c_b, d_mod_all, DOWN)
    d_cond_part = dot(d_mod_all, mod_b, ACROSS) * silu_slope(cond)
    d_silu_t_part = lax.dot_general(d_cond_part, time2_b.astype(F32), ALONG, precision=HIGH)
    thick = jnp.concatenate([d_silu_t_part.T, d_patch, d_head], 1)
    thick = fc_way.step(at_way.step(thick))
    thick = jnp.sum(exchange(thick.reshape(n_dp, rows, -1), "dp"), 0)
    thick = sum_all(jnp.concatenate([thick, d_cond_part.T], 1), "mp")
    d_silu_t = thick[:, :slots_all].T
    g_patch = thick[:, slots_all : slots_all + PIN]
    g_head = thick[:, slots_all + PIN : slots_all + 2 * PIN]
    d_cond = thick[:, slots_all + 2 * PIN :]
    g_table = lax.dot_general(d_cond, onehot, ALONG, precision=HIGH)
    g_time2 = lax.dot_general(d_cond, silu_t_b.astype(F32), ALONG, precision=HIGH)
    d_hidden = d_silu_t * silu_slope(hidden_t)
    g_time1 = lax.dot_general(d_hidden, feat_b.astype(F32), DOWN, precision=HIGH)
    g_cond = jnp.concatenate([g_patch, g_time1, g_time2, g_table], 1)

    sum_at = at_way.finish()
    at_way = Course(gather_steps(sum_at.astype(LOW), "dp"))

    square = lambda g: jnp.sum(g * g)
    split_sq = square(sum_fc) + square(sum_at) + square(g_mod)
    shared = sum_all(jnp.stack([split_sq, loss_part]), "mp")
    tally = jnp.stack([shared[0] + square(g_head) + square(g_cond), shared[1]])
    tally = fc_way.step(at_way.step(jnp.broadcast_to(tally[:, None], (2, 128))))
    tally = jnp.sum(spread(tally, "dp"), 0)
    grad_norm = jnp.sqrt(tally[0, 0])
    loss_sum = tally[1, 0]
    coef = jnp.minimum(1.0, CLIP / (grad_norm + 1e-06))

    all_fc = fc_way.finish()
    all_at = at_way.finish()
    near = me % 2
    own = ((me // 2) * (2 * rows))[None].astype(jnp.int32)
    factor = coef[None]
    rows_of_block = functools.partial(muon_rows, own, 2 * rows, factor, old)

    def one_mod():
        return rows_of_block(0, (silu_c_all, d_mod_all), 0, 8 * width, (0, 8 * width))

    def both_fc():
        base = 8 * width // hidden
        return jnp.concatenate(
            [rows_of_block(base + k, (all_fc,), k, hidden, (0, hidden)) for k in range(2)], 1
        )

    last = (8 * width + 2 * hidden) // (4 * width)

    def one_qkv():
        return rows_of_block(last, (all_at,), 0, 4 * width, (0, 3 * width))

    def one_out():
        mine = rows_of_block(last, (all_at,), 0, 4 * width, (3 * width, 4 * width))
        return jnp.pad(mine, ((0, 0), (0, 2 * width)))

    def shared_rows(both):
        mine = lax.dynamic_slice_in_dim(both, near * rows, rows, 0)
        theirs = lax.dynamic_slice_in_dim(both, (1 - near) * rows, rows, 0)
        theirs = swap(theirs, "dp", 1)
        return jnp.where(near == 0, mine, theirs), jnp.where(near == 0, theirs, mine)

    u_mod, u_fc = shared_rows(lax.cond(near == 0, one_mod, both_fc))
    u_qkv, u_out = shared_rows(lax.cond(near == 0, one_qkv, one_out))
    masters = (w_qkv, w_out, w_fc1, w_fc2, w_mod)
    old_moms = (mom_qkv, mom_out, mom_fc1, mom_fc2, mom_mod)
    fresh = (sum_at[:, : 3 * width], sum_at[:, 3 * width :], sum_fc[:, :hidden], sum_fc[:, hidden:], g_mod)
    updates = (u_qkv, u_out[:, :width], u_fc[:, :hidden], u_fc[:, hidden:], u_mod)
    new_weights = [
        w * (1.0 - LR_MUON * DECAY) - LR_MUON * u.astype(F32).reshape(w.shape) for w, u in zip(masters, updates)
    ]
    new_moms = [MU * m + coef * g.reshape(m.shape) for m, g in zip(old_moms, fresh)]

    adam_out = []
    for master, first, second, grad in (
        (w_head, first_head, second_head, g_head),
        (w_cond, first_cond, second_cond, g_cond),
    ):
        clipped = coef * grad
        first = BETA_ONE * first + (1.0 - BETA_ONE) * clipped
        second = BETA_TWO * second + (1.0 - BETA_TWO) * clipped * clipped
        update = first / (1.0 - BETA_ONE**STEP) / (jnp.sqrt(second / (1.0 - BETA_TWO**STEP)) + EPS_ADAM)
        adam_out.append((master - LR_ADAM * (update + DECAY * master), first, second))
    return (
        *new_weights,
        adam_out[0][0],
        adam_out[1][0],
        *new_moms,
        adam_out[0][1],
        adam_out[0][2],
        adam_out[1][1],
        adam_out[1][2],
        loss_sum,
        weight_total,
        grad_norm,
    )


def solution(mesh):
    row, wide, cube = P("dp", None), P("dp", "mp"), P("dp", None, "mp")
    in_specs = (
        *(row, row, P("dp"), row, row),
        *(cube, wide, wide, wide, cube, row, row),
        *(cube, wide, wide, wide, cube),
        *(row, row, row, row),
    )
    out_specs = (
        *(cube, wide, wide, wide, cube, row, row),
        *(cube, wide, wide, wide, cube),
        *(row, row, row, row),
        *(P(), P(), P()),
    )
    return jax.shard_map(body, mesh=mesh, in_specs=in_specs, out_specs=out_specs, check_vma=False)
```

time: 907 us -> 585 us (0.64)
  matrix products: 359 us -> 43.3 us
  Pallas kernels: 0 us -> 66.4 us
  waiting for transfers between devices: 240 us -> 183 us
  blocking collectives: 23.9 us -> 0 us
  starting transfers between devices: 53.5 us -> 66.8 us
    dot_general x74 -> x23, matrix products: 293 us -> 41.1 us  [dot(): return lax.dot_general(a, b, dims, preferred_element_type=F32)]
    ppermute x34 -> x40, waiting for transfers between devices: 202 us -> 134 us  [swap(): return lax.ppermute(x, axis, [(i, i ^ bit) for i in range(size)])]
    pallas_call x0 -> x4, Pallas kernels: none -> 66.4 us  [the longest x2 43.7 us: muon_rows(): pl.pallas_call(functools.partial(muon_kernel, tile, columns), grid=(1,),...]
    dot_general x6 -> x0, matrix products: 63.8 us -> none  [the longest x1 21.2 us: attend_back(): jnp.einsum('hqk,hkd->hqd', d_score, key, preferred_element_type=F32)]
    add x1, other arithmetic: 24.3 us -> 0.7 us  [body(): h_fin = (unit3 * (1.0 + mods[7]) + mods[6]).astype(LOW)]
    all_gather x1 -> x0, blocking collectives: 13.1 us -> none  [body(): mod = lax.all_gather(mod_cols, 'mp', axis=2, tiled=True)]
    psum x1 -> x0, blocking collectives: 10.8 us -> none  [body(): shared = lax.psum(jnp.stack([split_sq, loss_part]), 'mp')]
    all_gather x1, waiting for transfers between devices: 6.92 us -> 17.3 us  [body(): old = lax.all_gather(after(old, mixed_b), 'dp', axis=0, tiled=True)]
  transfers between devices with their start and end apart: 42 -> 49, of which waited for: 30 -> 28; matrix products, arithmetic and copies ran while one was open for 24% -> 30% of each run, Pallas kernels for 0% -> 10%
where the time goes in v2:
time: 585 us; the launch traced here: 575 us
  waiting for transfers between devices  183 us (31%)
  other arithmetic  103 us (18%)
  local copies, waits for them, and re-layouts  74.8 us (13%)
  starting transfers between devices  66.8 us (11%)
  Pallas kernels  66.4 us (11%)
  matrix products  43.3 us (7%)
  between operations  29.8 us (5%)
  loops' own time  8.03 us (1%)
    ppermute x40, waiting for transfers between devices, swap(): return lax.ppermute(x, axis, [(i, i ^ bit) for i in range(size)])  134 us
    pallas_call x2, Pallas kernels, muon_rows(): pl.pallas_call(functools.partial(muon_kernel, tile, columns), grid=(1,),...  43.7 us
    dot_general x23, matrix products, dot(): return lax.dot_general(a, b, dims, preferred_element_type=F32)  41.1 us
    ppermute x40, starting transfers between devices, swap(): return lax.ppermute(x, axis, [(i, i ^ bit) for i in range(size)])  30.9 us
    select_n x27, other arithmetic, gather_steps(): jnp.where(low_half, jnp.stack([cur, other], 1), jnp.stack([other, cur], 1))  29.9 us
    all_to_all x4, starting transfers between devices, spread(): return lax.all_to_all(copies, axis, 0, 0, tiled=True)  21.3 us
    all_to_all x4, waiting for transfers between devices, exchange(): return lax.all_to_all(x, axis, 0, 0, tiled=True)  20.4 us
    unnamed x212, local copies, waits for them, and re-layouts  20 us
  transfers between devices with their start and end apart: 49, of which 28 were waited for; matrix products, arithmetic and copies ran while one was open for 30% of the time, Pallas kernels for 10%

profile of v2, /device:TPU:0, one launch (start us, length us, event | category | flops | bytes accessed | tf_op | source)
XLA Modules:
  0.0 574.6 jit_solution(331102781917438462)
XLA Ops:
  17.2 6.1 %all-to-all-start = ((f32[8,104,32]{1,2,0:T(8,128)}), f32[8,104,32]{1,2,0:T(8,128)S(1)}, u32[]{:S(2)}, u32[]{:S(2)}) async-start(f32[8,104,32]{1,2,0:T(8,128)} %broadcast_in_dim.194), calls=%async_computation | async-start | bytes 262144 | tf_op jit(solution)/shard_map/all_to_all | solution.py:127
  29.2 8.4 %collective-permute-done = bf16[1,96,576]{1,2,0:T(8,128)(2,1)S(1)} collective-permute-done((bf16[1,96,576]{1,2,0:T(8,128)(2,1)S(1)}, bf16[1,96,576]{1,2,0:T(8,128)(2,1)S(1)}, u32[]{:S(2)}, u32[]{:S(2)}) %collective-permute-start) | collective-permute-done | bytes 110624 | tf_op jit(solution)/shard_map/ppermute | solution.py:45
  61.8 14.2 %all-to-all-done.2 = f32[8,4,1536]{2,1,0:T(4,128)S(1)} async-done(((f32[8,4,1536]{2,1,0:T(4,128)}), f32[8,4,1536]{2,1,0:T(4,128)S(1)}, u32[]{:S(2)}, u32[]{:S(2)}) %all-to-all-start.2) | async-done | bytes 196640 | tf_op jit(solution)/shard_map/all_to_all | solution.py:131
  91.4 5.6 collective-permute-done.4
  108.5 21.8 %collective-permute-done.7 = bf16[4,96,1728]{2,1,0:T(8,128)(2,1)} collective-permute-done((bf16[4,96,1728]{2,1,0:T(8,128)(2,1)S(1)}, bf16[4,96,1728]{2,1,0:T(8,128)(2,1)}, u32[]{:S(2)}, u32[]{:S(2)}) %collective-permute-start.7) | collective-permute-done | bytes 1327136 | tf_op jit(solution)/shard_map/ppermute | solution.py:45
  132.7 10.6 %attend.1 = (bf16[1024,192]{1,0:T(8,128)(2,1)S(1)}, f32[8,1024]{1,0:T(8,128)S(1)}) custom-call(s32[1]{0:T(128)} %bitcast.19.single_ref, bf16[1024,576]{1,0:T(8,128)(2,1)S(1)} %convolution_convert_fusion.qkv_ref), custom_call_target="tpu_custom_call" | custom-call | flops 805306368 | bytes 1572864 | tf_op jit(solution)/shard_map/attend/pallas_call | solution.py:240
  168.3 8.5 %collective-permute-done.10 = bf16[1,256,768]{2,1,0:T(8,128)(2,1)S(1)} collective-permute-done((bf16[1,256,768]{2,1,0:T(8,128)(2,1)S(1)}, bf16[1,256,768]{2,1,0:T(8,128)(2,1)S(1)}, u32[]{:S(2)}, u32[]{:S(2)}) %collective-permute-start.10) | collective-permute-done | bytes 393248 | tf_op jit(solution)/shard_map/ppermute | solution.py:45
  181.9 9.8 %multiply_convert_fusion = (bf16[1024,768]{1,0:T(8,128)(2,1)S(1)}, f32[1024,768]{1,0:T(8,128)}, f32[1024,768]{1,0:T(8,128)}) fusion(bf16[1024,768]{1,0:T(8,128)(2,1)S(1)} %bitcast.309, bf16[768,1728]{1,0:T(8,128)(2,1)S(1)} %bitcast.297), kind=kOutput, calls=%fused_computation.6 | convolution fusion | flops 1259077632 | bytes 10616832 | tf_op jit(solution)/shard_map/dot_general | solution.py:40
  202.5 6.8 %collective-permute-done.13 = bf16[1,256,768]{2,1,0:T(8,128)(2,1)} collective-permute-done((bf16[1,256,768]{2,1,0:T(8,128)(2,1)}, bf16[1,256,768]{2,1,0:T(8,128)(2,1)}, u32[]{:S(2)}, u32[]{:S(2)}) %collective-permute-start.13) | collective-permute-done | bytes 393248 | tf_op jit(solution)/shard_map/ppermute | solution.py:45
  219.3 8.6 %collective-permute-done.14 = bf16[1,256,768]{2,1,0:T(8,128)(2,1)S(1)} collective-permute-done((bf16[1,256,768]{2,1,0:T(8,128)(2,1)S(1)}, bf16[1,256,768]{2,1,0:T(8,128)(2,1)S(1)}, u32[]{:S(2)}, u32[]{:S(2)}) %collective-permute-start.14) | collective-permute-done | bytes 393248 | tf_op jit(solution)/shard_map/ppermute | solution.py:45
  235.2 17.3 %all-gather.2.cloned.1.call-done = bf16[768,3840]{1,0:T(8,128)(2,1)} async-done(((bf16[96,3840]{1,0:T(8,128)(2,1)}), bf16[768,3840]{1,0:T(8,128)(2,1)}) %all-gather.2.cloned.1.call-update) | async-done | bytes 5898256 | tf_op jit(solution)/shard_map/all_gather | solution.py:555
  268.1 6.2 %copy.366 = f32[768,1536]{1,0:T(8,128)} copy(f32[768,1536]{0,1:T(8,128)} %pad_maximum_fusion.1) | data formatting | bytes 9437184 | tf_op jit(solution)/shard_map/concatenate | solution.py:562
  289.4 18.9 %collective-permute-done.16 = bf16[4,96,1536]{2,1,0:T(8,128)(2,1)} collective-permute-done((bf16[4,96,1536]{2,1,0:T(8,128)(2,1)}, bf16[4,96,1536]{2,1,0:T(8,128)(2,1)}, u32[]{:S(2)}, u32[]{:S(2)}) %collective-permute-start.16) | collective-permute-done | bytes 1179680 | tf_op jit(solution)/shard_map/ppermute | solution.py:45
  315.3 9.8 %collective-permute-done.17 = bf16[2,96,1536]{2,1,0:T(8,128)(2,1)S(1)} collective-permute-done((bf16[2,96,1536]{2,1,0:T(8,128)(2,1)S(1)}, bf16[2,96,1536]{2,1,0:T(8,128)(2,1)S(1)}, u32[]{:S(2)}, u32[]{:S(2)}) %collective-permute-start.17) | collective-permute-done | bytes 589856 | tf_op jit(solution)/shard_map/ppermute | solution.py:45
  335.1 6.0 %collective-permute-done.18 = bf16[1,96,1536]{2,1,0:T(8,128)(2,1)} collective-permute-done((bf16[1,96,1536]{2,1,0:T(8,128)(2,1)}, bf16[1,96,1536]{2,1,0:T(8,128)(2,1)}, u32[]{:S(2)}, u32[]{:S(2)}) %collective-permute-start.18) | collective-permute-done | bytes 294944 | tf_op jit(solution)/shard_map/ppermute | solution.py:45
  347.9 12.1 %attend_back.1 = bf16[1024,576]{1,0:T(8,128)(2,1)S(1)} custom-call(s32[1]{0:T(128)} %bitcast.19.single_ref, bf16[1024,576]{1,0:T(8,128)(2,1)S(1)} %convolution_convert_fusion.qkv_ref, bf16[1024,192]{1,0:T(8,128)(2,1)S(1)} %convolution_convert_fusion.1.grad_ref, f32[8,1024]{1,0:T(8,128)S(1)} %get-tuple-element.113.total_ref), custom_call_target="tpu_custom_call" | custom-call | flops 2013265920 | bytes 2752512 | tf_op jit(solution)/shard_map/attend_back/pallas_call | solution.py:316
  373.2 9.5 %collective-permute-done.23 = bf16[4,96,768]{2,1,0:T(8,128)(2,1)S(1)} collective-permute-done((bf16[4,96,768]{2,1,0:T(8,128)(2,1)S(1)}, bf16[4,96,768]{2,1,0:T(8,128)(2,1)S(1)}, u32[]{:S(2)}, u32[]{:S(2)}) %collective-permute-start.23) | collective-permute-done | bytes 589856 | tf_op jit(solution)/shard_map/ppermute | solution.py:45
  394.2 6.4 %collective-permute-done.25 = bf16[1,96,768]{2,1,0:T(8,128)(2,1)S(1)} collective-permute-done((bf16[1,96,768]{2,1,0:T(8,128)(2,1)S(1)}, bf16[1,96,768]{2,1,0:T(8,128)(2,1)S(1)}, u32[]{:S(2)}, u32[]{:S(2)}) %collective-permute-start.25) | collective-permute-done | bytes 147488 | tf_op jit(solution)/shard_map/ppermute | solution.py:45
  426.7 6.2 %all-to-all-start.5 = ((bf16[8,4,2304]{2,1,0:T(4,128)(2,1)}), bf16[8,4,2304]{2,1,0:T(4,128)(2,1)}, u32[]{:S(2)}, u32[]{:S(2)}) async-start(bf16[8,4,2304]{2,1,0:T(4,128)(2,1)} %broadcast_in_dim.216), calls=%async_computation.5 | async-start | bytes 294912 | tf_op jit(solution)/shard_map/all_to_all | solution.py:127
  434.6 5.9 %all-to-all-done.5 = bf16[8,4,2304]{2,1,0:T(4,128)(2,1)} async-done(((bf16[8,4,2304]{2,1,0:T(4,128)(2,1)}), bf16[8,4,2304]{2,1,0:T(4,128)(2,1)}, u32[]{:S(2)}, u32[]{:S(2)}) %all-to-all-start.5) | async-done | bytes 147488 | tf_op jit(solution)/shard_map/all_to_all | solution.py:127
  493.7 36.0 %conditional.3 = (bf16[192,1536]{1,0:T(8,128)(2,1)S(1)}) conditional(s32[]{:T(128)} %convert_element_type.347, (pred[]{:T(512)}, bf16[4,2,96,1536]{3,2,1,0:T(8,128)(2,1)}, bf16[4,2,96,1536]{3,2,1,0:T(8,128)(2,1)S(1)}, s32[1]{0:T(128)}, f32[1]{0:T(128)}, /*index=5*/bf16[768,3840]{1,0:T(8,128)(2,1)}) %tuple.51, (bf16[8,96,32]{1,2,0:T(8,128)(2,1)S(1)}, ...), branch_computations={%region_38.39_spmd, %region_39.40_spmd} | conditional | flops 27181449216 | bytes 38928420 | solution.py:652
  501.7 28.0 %muon.9 = bf16[192,1536]{1,0:T(8,128)(2,1)S(1)} custom-call(s32[1]{0:T(128)} %get-tuple-element.63.own_ref, f32[1]{0:T(128)} %get-tuple-element.64.coef_ref, bf16[768,3840]{1,0:T(8,128)(2,1)} %get-tuple-element.65.mom_ref, bf16[768,32]{1,0:T(8,128)(2,1)S(1)} %bitcast.276, bf16[32,1536]{1,0:T(8,128)(2,1)S(1)} %get-tuple-element.67.refs_1_), custom_call_target="tpu_custom_call" | custom-call | flops 22649241600 | bytes 7077888 | tf_op jit(solution)/shard_map/cond/branch_1_fun/muon/pallas_call | solution.py:413
  538.7 16.1 %conditional.2 = (bf16[192,576]{0,1:T(8,128)(2,1)S(1)}) conditional(s32[]{:T(128)} %convert_element_type.347, (s32[1]{0:T(128)}, f32[1]{0:T(128)}, bf16[768,3840]{1,0:T(8,128)(2,1)}, bf16[768,768]{1,0:T(8,128)(2,1)S(1)}) %tuple.126, (s32[1]{0:T(128)}, f32[1]{0:T(128)}, bf16[768,3840]{1,0:T(8,128)(2,1)}, bf16[768,768]{1,0:T(8,128)(2,1)S(1)}) %tuple.127), branch_computations={%region_36.37_spmd, %region_37.38_spmd} | conditional | flops 11324620800 | bytes 3096584 | solution.py:653
  538.9 15.7 %muon.6 = bf16[192,576]{1,0:T(8,128)(2,1)S(1)} custom-call(s32[1]{0:T(128)} %get-tuple-element.53.own_ref, f32[1]{0:T(128)} %get-tuple-element.54.coef_ref, bf16[768,3840]{1,0:T(8,128)(2,1)} %get-tuple-element.55.mom_ref, bf16[768,768]{1,0:T(8,128)(2,1)S(1)} %get-tuple-element.56.refs_0_), custom_call_target="tpu_custom_call" | custom-call | flops 11324620800 | bytes 2654208 | tf_op jit(solution)/shard_map/cond/branch_1_fun/muon/pallas_call | solution.py:413
  (565 shorter events, 294.2 us)
Async XLA Ops:
  9.6 44.9 %collective-permute-start.2 = (bf16[1,96,1728]{2,1,0:T(8,128)(2,1)S(1)}, bf16[1,96,1728]{2,1,0:T(8,128)(2,1)S(1)}, u32[]{:S(2)}, u32[]{:S(2)}) collective-permute-start(bf16[1,96,1728]{2,1,0:T(8,128)(2,1)S(1)} %concatenate.255), channel_id=1, source_target_pairs={{0,16},{4,20},{8,24},{12,28},{16,0},{20,4},{24,8},{28,12},{1,17},{... | collective-permute-start | bytes 995336 | tf_op jit(solution)/shard_map/ppermute | solution.py:45
  14.8 22.7 %collective-permute-start = (bf16[1,96,576]{1,2,0:T(8,128)(2,1)S(1)}, bf16[1,96,576]{1,2,0:T(8,128)(2,1)S(1)}, u32[]{:S(2)}, u32[]{:S(2)}) collective-permute-start(bf16[1,96,576]{1,2,0:T(8,128)(2,1)S(1)} %bitcast.317), channel_id=1, source_target_pairs={{0,16},{4,20},{8,24},{12,28},{16,0},{20,4},{24,8},{28,12},{1,17},{... | collective-permute-start | bytes 331784 | tf_op jit(solution)/shard_map/ppermute | solution.py:45
  17.2 22.4 %all-to-all-start = ((f32[8,104,32]{1,2,0:T(8,128)}), f32[8,104,32]{1,2,0:T(8,128)S(1)}, u32[]{:S(2)}, u32[]{:S(2)}) async-start(f32[8,104,32]{1,2,0:T(8,128)} %broadcast_in_dim.194), calls=%async_computation | async-start | bytes 262144 | tf_op jit(solution)/shard_map/all_to_all | solution.py:127
  38.4 18.4 %collective-permute-start.1 = (bf16[2,96,576]{1,2,0:T(8,128)(2,1)}, bf16[2,96,576]{1,2,0:T(8,128)(2,1)S(1)}, u32[]{:S(2)}, u32[]{:S(2)}) collective-permute-start(bf16[2,96,576]{1,2,0:T(8,128)(2,1)} %maximum_select_fusion.21), channel_id=1, source_target_pairs={{0,8},{4,12},{8,0},{12,4},{16,24},{20,28},{24,16},{28,20},{1,9},{5... | collective-permute-start | bytes 663560 | tf_op jit(solution)/shard_map/ppermute | solution.py:45
  55.5 20.6 %collective-permute-start.3 = (bf16[2,96,1728]{2,1,0:T(8,128)(2,1)}, bf16[2,96,1728]{2,1,0:T(8,128)(2,1)S(1)}, u32[]{:S(2)}, u32[]{:S(2)}) collective-permute-start(bf16[2,96,1728]{2,1,0:T(8,128)(2,1)} %maximum_select_fusion.15), channel_id=1, source_target_pairs={{0,8},{4,12},{8,0},{12,4},{16,24},{20,28},{24,16},{28,20},{1,9},{5... | collective-permute-start | bytes 1990664 | tf_op jit(solution)/shard_map/ppermute | solution.py:45
  57.5 18.5 %all-to-all-start.2 = ((f32[8,4,1536]{2,1,0:T(4,128)}), f32[8,4,1536]{2,1,0:T(4,128)S(1)}, u32[]{:S(2)}, u32[]{:S(2)}) async-start(f32[8,4,1536]{2,1,0:T(4,128)} %reshape.1308), calls=%async_computation.2 | async-start | bytes 393216 | tf_op jit(solution)/shard_map/all_to_all | solution.py:131
  80.2 172.3 %all-gather.2.cloned.1.call-start = ((), (), s32[]{:S(2)}) async-start(), calls=%async_computation.8 | async-start | bytes 6635520 | tf_op jit(solution)/shard_map/all_gather | solution.py:555
  87.7 14.4 %collective-permute-start.6 = (bf16[4,96,576]{2,1,0:T(8,128)(2,1)}, bf16[4,96,576]{2,1,0:T(8,128)(2,1)}, u32[]{:S(2)}, u32[]{:S(2)}) collective-permute-start(bf16[4,96,576]{2,1,0:T(8,128)(2,1)} %copy.353), channel_id=1, source_target_pairs={{0,4},{4,0},{8,12},{12,8},{16,20},{20,16},{24,28},{28,24},{1,5},{5... | collective-permute-start | bytes 1327112 | tf_op jit(solution)/shard_map/ppermute | solution.py:45
  89.3 41.0 %collective-permute-start.7 = (bf16[4,96,1728]{2,1,0:T(8,128)(2,1)S(1)}, bf16[4,96,1728]{2,1,0:T(8,128)(2,1)}, u32[]{:S(2)}, u32[]{:S(2)}) collective-permute-start(bf16[4,96,1728]{2,1,0:T(8,128)(2,1)S(1)} %bitcast.288), channel_id=1, source_target_pairs={{0,4},{4,0},{8,12},{12,8},{16,20},{20,16},{24,28},{28,24},{1,5},{5... | collective-permute-start | bytes 3981320 | tf_op jit(solution)/shard_map/ppermute | solution.py:45
  279.6 28.7 %collective-permute-start.16 = (bf16[4,96,1536]{2,1,0:T(8,128)(2,1)}, bf16[4,96,1536]{2,1,0:T(8,128)(2,1)}, u32[]{:S(2)}, u32[]{:S(2)}) collective-permute-start(bf16[4,96,1536]{2,1,0:T(8,128)(2,1)} %fusion.6), channel_id=1, source_target_pairs={{0,4},{4,0},{8,12},{12,8},{16,20},{20,16},{24,28},{28,24},{1,5},{5... | collective-permute-start | bytes 3538952 | tf_op jit(solution)/shard_map/ppermute | solution.py:45
  287.8 22.5 %collective-permute-start.20 = (bf16[1,256,768]{2,1,0:T(8,128)(2,1)S(1)}, bf16[1,256,768]{2,1,0:T(8,128)(2,1)S(1)}, u32[]{:S(2)}, u32[]{:S(2)}) collective-permute-start(bf16[1,256,768]{2,1,0:T(8,128)(2,1)S(1)} %dynamic-slice_convert_fusion.4), channel_id=1, source_target_pairs={{0,2},{1,3},{2,0},{3,1},{4,6},{5,7},{6,4},{7,5},{8,10},{9,11},{10,... | collective-permute-start | bytes 1179656 | tf_op jit(solution)/shard_map/ppermute | solution.py:45
  310.0 15.0 %collective-permute-start.17 = (bf16[2,96,1536]{2,1,0:T(8,128)(2,1)S(1)}, bf16[2,96,1536]{2,1,0:T(8,128)(2,1)S(1)}, u32[]{:S(2)}, u32[]{:S(2)}) collective-permute-start(bf16[2,96,1536]{2,1,0:T(8,128)(2,1)S(1)} %fusion.30), channel_id=1, source_target_pairs={{0,8},{4,12},{8,0},{12,4},{16,24},{20,28},{24,16},{28,20},{1,9},{5... | collective-permute-start | bytes 1769480 | tf_op jit(solution)/shard_map/ppermute | solution.py:45
  313.8 19.8 %collective-permute-start.21 = (bf16[1,256,768]{2,1,0:T(8,128)(2,1)}, bf16[1,256,768]{2,1,0:T(8,128)(2,1)S(1)}, u32[]{:S(2)}, u32[]{:S(2)}) collective-permute-start(bf16[1,256,768]{2,1,0:T(8,128)(2,1)} %get-tuple-element.310), channel_id=1, source_target_pairs={{0,2},{1,3},{2,0},{3,1},{4,6},{5,7},{6,4},{7,5},{8,10},{9,11},{10,... | collective-permute-start | bytes 1179656 | tf_op jit(solution)/shard_map/ppermute | solution.py:45
  326.0 15.1 %collective-permute-start.18 = (bf16[1,96,1536]{2,1,0:T(8,128)(2,1)}, bf16[1,96,1536]{2,1,0:T(8,128)(2,1)}, u32[]{:S(2)}, u32[]{:S(2)}) collective-permute-start(bf16[1,96,1536]{2,1,0:T(8,128)(2,1)} %dynamic-slice_convert_fusion.8), channel_id=1, source_target_pairs={{0,16},{4,20},{8,24},{12,28},{16,0},{20,4},{24,8},{28,12},{1,17},{... | collective-permute-start | bytes 884744 | tf_op jit(solution)/shard_map/ppermute | solution.py:45
  342.9 24.6 %collective-permute-start.30 = (bf16[1,96,1536]{2,1,0:T(8,128)(2,1)}, bf16[1,96,1536]{2,1,0:T(8,128)(2,1)}, u32[]{:S(2)}, u32[]{:S(2)}) collective-permute-start(bf16[1,96,1536]{2,1,0:T(8,128)(2,1)} %fusion.33), channel_id=1, source_target_pairs={{0,16},{4,20},{8,24},{12,28},{16,0},{20,4},{24,8},{28,12},{1,17},{... | collective-permute-start | bytes 884744 | tf_op jit(solution)/shard_map/ppermute | solution.py:45
  367.5 15.3 %collective-permute-start.23 = (bf16[4,96,768]{2,1,0:T(8,128)(2,1)S(1)}, bf16[4,96,768]{2,1,0:T(8,128)(2,1)S(1)}, u32[]{:S(2)}, u32[]{:S(2)}) collective-permute-start(bf16[4,96,768]{2,1,0:T(8,128)(2,1)S(1)} %fusion.31), channel_id=1, source_target_pairs={{0,4},{4,0},{8,12},{12,8},{16,20},{20,16},{24,28},{28,24},{1,5},{5... | collective-permute-start | bytes 1769480 | tf_op jit(solution)/shard_map/ppermute | solution.py:45
  369.0 16.3 %collective-permute-start.34 = (bf16[2,96,1536]{2,1,0:T(8,128)(2,1)S(1)}, bf16[2,96,1536]{2,1,0:T(8,128)(2,1)S(1)}, u32[]{:S(2)}, u32[]{:S(2)}) collective-permute-start(bf16[2,96,1536]{2,1,0:T(8,128)(2,1)S(1)} %maximum_select_fusion.18), channel_id=1, source_target_pairs={{0,8},{4,12},{8,0},{12,4},{16,24},{20,28},{24,16},{28,20},{1,9},{5... | collective-permute-start | bytes 1769480 | tf_op jit(solution)/shard_map/ppermute | solution.py:45
  373.2 18.1 %collective-permute-start.26 = (bf16[2,256,768]{2,1,0:T(8,128)(2,1)S(1)}, bf16[2,256,768]{2,1,0:T(8,128)(2,1)S(1)}, u32[]{:S(2)}, u32[]{:S(2)}) collective-permute-start(bf16[2,256,768]{2,1,0:T(8,128)(2,1)S(1)} %fusion.21), channel_id=1, source_target_pairs={{0,1},{1,0},{2,3},{3,2},{4,5},{5,4},{6,7},{7,6},{8,9},{9,8},{10,11... | collective-permute-start | bytes 2359304 | tf_op jit(solution)/shard_map/ppermute | solution.py:45
  385.4 89.7 %collective-permute-start.38 = (bf16[4,96,1536]{2,1,0:T(8,128)(2,1)S(1)}, bf16[4,96,1536]{2,1,0:T(8,128)(2,1)}, u32[]{:S(2)}, u32[]{:S(2)}) collective-permute-start(bf16[4,96,1536]{2,1,0:T(8,128)(2,1)S(1)} %bitcast.291), channel_id=1, source_target_pairs={{0,4},{4,0},{8,12},{12,8},{16,20},{20,16},{24,28},{28,24},{1,5},{5... | collective-permute-start | bytes 3538952 | tf_op jit(solution)/shard_map/ppermute | solution.py:45
  401.3 16.0 %collective-permute-start.33 = (bf16[1,96,768]{2,1,0:T(8,128)(2,1)}, bf16[1,96,768]{2,1,0:T(8,128)(2,1)}, u32[]{:S(2)}, u32[]{:S(2)}) collective-permute-start(bf16[1,96,768]{2,1,0:T(8,128)(2,1)} %fusion.50), channel_id=1, source_target_pairs={{0,16},{4,20},{8,24},{12,28},{16,0},{20,4},{24,8},{28,12},{1,17},{... | collective-permute-start | bytes 442376 | tf_op jit(solution)/shard_map/ppermute | solution.py:45
  419.2 43.0 %collective-permute-start.35 = (bf16[2,96,768]{2,1,0:T(8,128)(2,1)}, bf16[2,96,768]{2,1,0:T(8,128)(2,1)}, u32[]{:S(2)}, u32[]{:S(2)}) collective-permute-start(bf16[2,96,768]{2,1,0:T(8,128)(2,1)} %maximum_select_fusion.24), channel_id=1, source_target_pairs={{0,8},{4,12},{8,0},{12,4},{16,24},{20,28},{24,16},{28,20},{1,9},{5... | collective-permute-start | bytes 884744 | tf_op jit(solution)/shard_map/ppermute | solution.py:45
  426.7 13.9 %all-to-all-start.5 = ((bf16[8,4,2304]{2,1,0:T(4,128)(2,1)}), bf16[8,4,2304]{2,1,0:T(4,128)(2,1)}, u32[]{:S(2)}, u32[]{:S(2)}) async-start(bf16[8,4,2304]{2,1,0:T(4,128)(2,1)} %broadcast_in_dim.216), calls=%async_computation.5 | async-start | bytes 294912 | tf_op jit(solution)/shard_map/all_to_all | solution.py:127
  464.2 72.4 %collective-permute-start.36 = (bf16[4,96,768]{2,1,0:T(8,128)(2,1)}, bf16[4,96,768]{2,1,0:T(8,128)(2,1)}, u32[]{:S(2)}, u32[]{:S(2)}) collective-permute-start(bf16[4,96,768]{2,1,0:T(8,128)(2,1)} %bitcast.109), channel_id=1, source_target_pairs={{0,4},{4,0},{8,12},{12,8},{16,20},{20,16},{24,28},{28,24},{1,5},{5... | collective-permute-start | bytes 1769480 | tf_op jit(solution)/shard_map/ppermute | solution.py:45
  533.0 29.1 %collective-permute-start.39 = (bf16[96,1536]{1,0:T(8,128)(2,1)}, bf16[96,1536]{1,0:T(8,128)(2,1)S(1)}, u32[]{:S(2)}, u32[]{:S(2)}) collective-permute-start(bf16[96,1536]{1,0:T(8,128)(2,1)} %constant_dynamic-slice_fusion), channel_id=1, source_target_pairs={{0,4},{4,0},{8,12},{12,8},{16,20},{20,16},{24,28},{28,24},{1,5},{5... | collective-permute-start | bytes 884744 | tf_op jit(solution)/shard_map/ppermute | solution.py:45
  (128 other events, 1221.7 us)
Sparse Core Ops, SparseCore 0:
  161.6 90.8 all-gather.1
